TPU v7x, 32 devices: a whole 2x2x4 slice. The times are simulated.
32 devices in a mesh: dp: 8 (over y, x, core), expert: 4 (over z).
Axes of the slice: x: 2, y: 2, z: 4, core: 2. Of those that a mesh axis runs over, the one named last changes fastest.
Arguments:
- tokens: bfloat16 [4096, 1440], P(('dp', 'expert')), may hold values from -6 to 6
- expert_ids: int32 [4096, 2], P(('dp', 'expert')), may hold values from 0 to 3, all different within a row; in each aligned block of 128 rows (0 to 127, 128 to 255, ...) at most 128 rows name the same one
- combine_weights: float32 [4096, 2], P(('dp', 'expert')), may hold values from 0.2 to 1
- out_grad: bfloat16 [4096, 1440], P(('dp', 'expert')), may hold values from -6 to 6
- w_gate_up: bfloat16 [4, 1440, 2880], P('expert', 'dp'), may hold values from -0.15625 to 0.15625
- w_down: bfloat16 [4, 1440, 1440], P('expert', 'dp'), may hold values from -0.15625 to 0.15625
Outputs:
- mixed_out: bfloat16 [4096, 1440], P(('dp', 'expert'))
- token_grad: bfloat16 [4096, 1440], P(('dp', 'expert'))
- grad_gate_up: float32 [4, 1440, 2880], P('expert', 'dp')
- grad_down: float32 [4, 1440, 1440], P('expert', 'dp')
Inputs may be any that keep to these rules, and one draw needn't show every extreme that they name: `expert_ids`: each token names 2 different experts. The 128 tokens of one device name one expert at most 128 times, and in every draw some device names some expert exactly 128 times.
All inputs are finite; a program needn't handle non-finite values.
Results may differ from a plain program's by a relative error of at most 0.018.
Values may be sent and summed in bfloat16 or wider, within the bound.
No kernel may reach another device: no remote copies, remote signals or barrier semaphores. Data moves between devices by JAX's collectives and lax.ppermute only.
A program may use at most 192 MiB of HBM per device.

v0:
```python
import functools
import math

import jax
import jax.numpy as jnp
from jax import lax
from jax.experimental import pallas as pl
from jax.experimental.pallas import tpu as pltpu
from jax.sharding import PartitionSpec as P

GLU_ALPHA = 1.702
BF = jnp.bfloat16
F32 = jnp.float32


def route_matrix(expert_ids, combine_weights, experts):
    hit = expert_ids[:, :, None] == jnp.arange(experts, dtype=jnp.int32)[None, None, :]
    return jnp.sum(jnp.where(hit, combine_weights[:, :, None], 0.0), axis=1)


def dense_forward(rows, weight_gu):
    half = weight_gu.shape[1] // 2
    pre = jnp.dot(rows, weight_gu, preferred_element_type=F32)
    gate, up = pre[:, :half], pre[:, half:]
    sig = jax.nn.sigmoid(GLU_ALPHA * gate)
    glu = gate * sig
    hidden = ((up + 1.0) * glu).astype(BF)
    gate_factor = (up + 1.0) * (sig + GLU_ALPHA * gate * sig * (1.0 - sig))
    return hidden, glu, gate_factor


def contract(left, right, dims):
    return lax.dot_general(left, right, ((dims[:1], dims[1:]), ((), ())), preferred_element_type=F32)


def general(tokens, expert_ids, combine_weights, out_grad, w_gate_up, w_down):
    experts = lax.axis_size("expert")
    replicas = lax.axis_size("dp")
    count, top = expert_ids.shape
    scale = 1.0 / math.sqrt(replicas * count * top)
    me = lax.axis_index("expert")
    table = route_matrix(expert_ids, combine_weights, experts)
    rows = lax.all_gather(tokens, "expert", axis=0, tiled=True)
    grads = lax.all_gather(out_grad, "expert", axis=0, tiled=True)
    table = lax.all_gather(table, "expert", axis=0, tiled=True)
    weight = lax.dynamic_slice_in_dim(table, me, 1, 1)
    row_grad = (weight * grads.astype(F32)).astype(BF)
    weight_gu = lax.all_gather(w_gate_up[0], "dp", axis=0, tiled=True)
    weight_down = lax.all_gather(w_down[0], "dp", axis=0, tiled=True)
    hidden, glu, gate_factor = dense_forward(rows, weight_gu)
    expert_out = jnp.dot(hidden, weight_down, preferred_element_type=F32).astype(BF)
    mixed = (weight * expert_out.astype(F32)).astype(BF)
    hidden_grad = contract(row_grad, weight_down, (1, 1))
    pre_grad = jnp.concatenate([hidden_grad * gate_factor, hidden_grad * glu], axis=1).astype(BF)
    input_grad = contract(pre_grad, weight_gu, (1, 1)).astype(BF)
    part_gu = (contract(rows, pre_grad, (0, 0)) * scale).astype(BF)
    part_down = (contract(hidden, row_grad, (0, 0)) * scale).astype(BF)

    def scatter(value, axis):
        return lax.psum_scatter(value, axis, scatter_dimension=0, tiled=True)

    return (
        scatter(mixed, "expert"),
        scatter(input_grad, "expert"),
        scatter(part_gu, "dp").astype(F32)[None],
        scatter(part_down, "dp").astype(F32)[None],
    )


PAD = 192
HALF = 96
MAIN = 156
LOT = 80
MIB = 1024 * 1024
LONG = 30_000_000_000


def zeros(shape, dtype=F32):
    return jnp.zeros(shape, dtype)


def prepare_kernel(spot, tokens_t, grads_t, ids_t, weights_t, w_gu, w_down, x_out, g_out, own, other, low, high):
    core = spot[0]
    width, count = tokens_t.shape
    block = w_gu.shape[0]
    blocks = width // block
    gap = PAD - block
    full = blocks * PAD

    x = tokens_t[...].astype(F32)
    spread = []
    for i in range(blocks):
        spread += [x[i * block : (i + 1) * block], zeros((gap, count))]
    x_out[...] = jnp.concatenate(spread, axis=0).T.astype(BF)

    hit = [ids_t[...] == e for e in range(4)]
    table = jnp.concatenate(
        [jnp.sum(jnp.where(h, weights_t[...], 0.0), axis=0, keepdims=True) for h in hit], axis=0
    )
    coarse = table.astype(BF).astype(F32)
    rows = [grads_t[...].astype(F32), coarse, table - coarse, zeros((full - width - 8, count))]
    g_out[...] = jnp.concatenate(rows, axis=0).T.astype(BF)

    w = w_gu[...]
    lot = block - MAIN
    edge = zeros((block, lot // 3), BF)
    slim = zeros((block, lot // 6), BF)

    def half(parity):
        parts = []
        for j in range(blocks):
            at = (2 * j + parity) * block
            parts += [w[:, at : at + MAIN], edge, w[:, at + MAIN : at + MAIN + gap], slim, w[:, at + MAIN + gap : at + block]]
        return jnp.concatenate(parts, axis=1)

    even, odd = half(0), half(1)
    down = jnp.concatenate([w_down[...], zeros((block, full - width), BF)], axis=1)
    own[:block, :] = jnp.where(core == 0, even, odd)
    own[block:, :] = down[MAIN : MAIN + gap]
    other[...] = jnp.concatenate([jnp.where(core == 0, odd, even), zeros((gap, full), BF)], axis=0)
    low[...] = down[:LOT]
    high[...] = jnp.concatenate([down[LOT:MAIN], zeros((2 * LOT - MAIN, full), BF)], axis=0)


def join_kernel(other, w_down, out):
    block = w_down.shape[0]
    gap = PAD - block
    out[...] = other[...]
    side = zeros((gap, out.shape[1] - w_down.shape[1]), BF)
    out[block:, :] = jnp.concatenate([w_down[block - gap :, :], side], axis=1)


def start_all(copies):
    for c in copies:
        c.start()
    return copies


def wait_all(copies):
    for c in copies:
        c.wait()


def gate_up_copies(spot, owns, others, w_gu, sems):
    core, chip = spot[0], spot[1]
    copies = []
    for k in range(4):
        j = jnp.bitwise_xor(chip, k)
        for n, (ref, which) in enumerate(((owns[k], core), (others[k], 1 - core))):
            row = pl.multiple_of((2 * j + which) * PAD, PAD)
            copies.append(pltpu.make_async_copy(ref, w_gu.at[pl.ds(row, PAD)], sems.at[2 * k + n]))
    return copies


def down_copies(spot, owns, others, lows, highs, w_down, sems):
    chip = spot[1]
    copies = []
    for k in range(4):
        base = jnp.bitwise_xor(chip, k) * PAD
        parts = (
            (lows[k], 0, LOT),
            (highs[k], LOT, LOT),
            (owns[k].at[pl.ds(PAD - 16, 16)], 2 * LOT, 16),
            (others[k].at[pl.ds(PAD - 16, 16)], 2 * LOT + 16, 16),
        )
        for ref, at, size in parts:
            row = pl.multiple_of(base + at, 16)
            copies.append(pltpu.make_async_copy(ref, w_down.at[pl.ds(row, size)], sems.at[len(copies)]))
    return copies


def row_copies(pieces, starts, scratch, sems):
    count, wide = pieces[0].shape[0], scratch.shape[1]
    return [
        pltpu.make_async_copy(p.at[:, pl.ds(start, wide)], scratch.at[pl.ds(n * count, count)], sems.at[n])
        for n, (p, start) in enumerate(zip(pieces, starts))
    ]


def chunk_copies(source, target, step, sems, base=0):
    return [
        pltpu.make_async_copy(source.at[pl.ds(m, step)], target.at[pl.ds(m, step)], sems.at[base + m // step])
        for m in range(0, source.shape[0], step)
    ]


STEP = 256
X_AT = (0, 0, 0, 0, 0, 0, 0, 0)
G_AT = (0, 8 * PAD, 8 * PAD, 0, 0, 8 * PAD, 8 * PAD, 0)


def hidden_kernel(*refs):
    spot, owns, others, pieces = refs[0], refs[1:5], refs[5:9], refs[9:17]
    hid_out, up_out, gate_out = refs[17:20]
    w_gu, x, hid, up_f, gate_f, w_sems, x_sems, out_sems = refs[20:]
    gu = start_all(gate_up_copies(spot, owns, others, w_gu, w_sems))
    xs = start_all(row_copies(pieces, X_AT, x, x_sems))
    wait_all(gu)
    half = w_gu.shape[1] // 2
    per = STEP // pieces[0].shape[0]
    outs = [
        chunk_copies(a, b, STEP, out_sems, base)
        for a, b, base in ((hid, hid_out, 0), (up_f, up_out, 4), (gate_f, gate_out, 8))
    ]
    for n in range(x.shape[0] // STEP):
        at = pl.ds(n * STEP, STEP)
        wait_all(xs[n * per : (n + 1) * per])
        pre = jnp.dot(x[at, :], w_gu[...], preferred_element_type=F32)
        gate, up = pre[:, :half], pre[:, half:] + 1.0
        sig = jax.nn.sigmoid(GLU_ALPHA * gate)
        glu = gate * sig
        hid[at, :] = (up * glu).astype(BF)
        up_f[at, :] = glu.astype(BF)
        gate_f[at, :] = (up * (sig + GLU_ALPHA * glu * (1.0 - sig))).astype(BF)
        for group in outs:
            group[n].start()
    for group in outs:
        wait_all(group)


def scatter_copies(chip, part, stride, a_at, b_at, send_a, keep_a, send_b, keep_b, sems):
    size = send_a.shape[1]
    copies = []
    plan_a = ((1, send_a, 0), (3, send_a, 1), (0, keep_a, 0), (2, keep_a, 1))
    plan_b = ((2, send_b, 0), (3, send_b, 1), (0, keep_b, 0), (1, keep_b, 1))
    for at, plan in ((a_at, plan_a), (b_at, plan_b)):
        for rel, ref, slot in plan:
            row = jnp.bitwise_xor(chip, rel) * (stride * PAD) + at
            source = part.at[pl.ds(pl.multiple_of(row, HALF), size)]
            copies.append(pltpu.make_async_copy(source, ref.at[slot], sems.at[len(copies)]))
    return copies


def down_grad_kernel(scale, *refs):
    spot, hid_in, pieces = refs[0], refs[1], refs[2:10]
    grad_out, *parts = refs[10:15]
    hid, g, part, hid_sem, g_sems, grad_sems, part_sems = refs[15:]
    line, chip = spot[2], spot[1]
    gs = start_all(row_copies(pieces, G_AT, g, g_sems))
    load = pltpu.make_async_copy(hid_in, hid, hid_sem.at[0])
    load.start()
    full = g.shape[1]
    lane = lax.broadcasted_iota(jnp.int32, (STEP, 128), 1)
    picked = (lane == 32 + line) | (lane == 36 + line)
    per = STEP // pieces[0].shape[0]
    grads = chunk_copies(g, grad_out, STEP, grad_sems)
    for n in range(g.shape[0] // STEP):
        at = pl.ds(n * STEP, STEP)
        wait_all(gs[n * per : (n + 1) * per])
        edge = g[at, pl.ds(full - 128, 128)].astype(F32)
        weight = jnp.sum(jnp.where(picked, edge, 0.0), axis=1, keepdims=True)
        g[at, :] = (weight * g[at, :].astype(F32)).astype(BF)
        grads[n].start()
    load.wait()
    for m in range(0, part.shape[0], STEP):
        at = pl.ds(m, STEP)
        part[at, :] = (contract(hid[:, at], g[...], (0, 0)) * scale).astype(BF)
    outs = start_all(scatter_copies(chip, part, 1, 0, HALF, *parts, part_sems))
    wait_all(grads)
    wait_all(outs)


def row_outs(out, last, first, rest, own, sems):
    return [
        pltpu.make_async_copy(out.at[pl.ds(7 * last, last)], first, sems.at[0]),
        pltpu.make_async_copy(out.at[pl.ds(4 * last, 3 * last)], rest, sems.at[1]),
        pltpu.make_async_copy(out.at[pl.ds(0, 4 * last)], own, sems.at[2]),
    ]


def gate_grad_kernel(scale, *refs):
    spot, owns, others, lows, highs = refs[0], refs[1:5], refs[5:9], refs[9:13], refs[13:17]
    hid_in, grad_in, up_in, gate_in, pieces = refs[17], refs[18], refs[19], refs[20], refs[21:29]
    out_own, out_first, out_rest, pre_out, *parts = refs[29:37]
    w_down, hid, g, up_f, gate_f, out, pre_grad, x, part = refs[37:46]
    w_sems, in_sems, x_sems, row_sems, out_sems, part_sems = refs[46:]
    down = start_all(down_copies(spot, owns, others, lows, highs, w_down, w_sems))
    loads = [
        start_all(chunk_copies(a, b, STEP, in_sems, base))
        for a, b, base in ((hid_in, hid, 0), (grad_in, g, 4), (up_in, up_f, 8), (gate_in, gate_f, 12))
    ]
    xs = start_all(row_copies(pieces, X_AT, x, x_sems))
    wait_all(down)
    last = out.shape[0] // 8
    wait_all(loads[0])
    for n in (3, 2, 1, 0):
        at = pl.ds(n * STEP, STEP)
        out[at, :] = jnp.dot(hid[at, :], w_down[...], preferred_element_type=F32).astype(BF)
    outs = start_all(row_outs(out, last, out_first, out_rest, out_own, row_sems))
    half = w_down.shape[0]
    pres = chunk_copies(pre_grad, pre_out, STEP, out_sems)
    for n in range(g.shape[0] // STEP):
        at = pl.ds(n * STEP, STEP)
        wait_all([loads[1][n], loads[2][n], loads[3][n]])
        hidden_grad = contract(g[at, :], w_down[...], (1, 1))
        pre_grad[at, :half] = (hidden_grad * gate_f[at, :].astype(F32)).astype(BF)
        pre_grad[at, half:] = (hidden_grad * up_f[at, :].astype(F32)).astype(BF)
        pres[n].start()
    wait_all(xs)
    for m in range(0, part.shape[0], 2 * PAD):
        at = pl.ds(m, 2 * PAD)
        part[at, :] = (contract(x[:, at], pre_grad[:, :half], (0, 0)) * scale).astype(BF)
    outs += start_all(scatter_copies(spot[1], part, 2, 0, PAD, *parts, part_sems))
    wait_all(pres)
    wait_all(outs)


def up_grad_kernel(scale, *refs):
    spot, owns, others, pieces, pre_in = refs[0], refs[1:5], refs[5:9], refs[9:17], refs[17]
    in_own, in_first, in_rest, *parts = refs[18:25]
    w_gu, x, pre_grad, part, out, w_sems, x_sems, in_sems, out_sems, part_sems = refs[25:]
    loads = start_all(chunk_copies(pre_in, pre_grad, STEP, in_sems))
    xs = start_all(row_copies(pieces, X_AT, x, x_sems))
    gu = start_all(gate_up_copies(spot, owns, others, w_gu, w_sems))
    wait_all(loads)
    wait_all(xs)
    half = part.shape[1]
    for m in range(0, part.shape[0], 2 * PAD):
        at = pl.ds(m, 2 * PAD)
        part[at, :] = (contract(x[:, at], pre_grad[:, half:], (0, 0)) * scale).astype(BF)
    outs = start_all(scatter_copies(spot[1], part, 2, 0, PAD, *parts, part_sems))
    wait_all(gu)
    last = out.shape[0] // 8
    for n in (3, 2, 1, 0):
        at = pl.ds(n * STEP, STEP)
        out[at, :] = contract(pre_grad[at, :], w_gu[...], (1, 1)).astype(BF)
    outs += start_all(row_outs(out, last, in_first, in_rest, in_own, out_sems))
    wait_all(outs)


def finish_rows_kernel(spread, keep, got, out_t):
    width = out_t.shape[0]
    total = (keep[...].astype(F32) + got[...].astype(F32)).T
    if spread:
        block = width // 8
        total = jnp.concatenate([total[i * PAD : i * PAD + block] for i in range(8)], axis=0)
    out_t[...] = total[:width].astype(BF)


def finish_gate_up_kernel(spot, gate_keep, gate_far, up_keep, up_far, out):
    core = spot[0]
    block = out.shape[0]
    parts = []
    for keep, far in ((gate_keep, gate_far), (up_keep, up_far)):
        mine = keep[...].astype(F32)[:block]
        theirs = far[...].astype(F32)[:block]
        even = jnp.where(core == 0, mine, theirs)
        odd = jnp.where(core == 0, theirs, mine)
        for j in range(4):
            for p in (even, odd):
                at = j * PAD
                parts += [p[:, at : at + MAIN], p[:, at + 164 : at + 176], p[:, at + 180 : at + PAD]]
    out[...] = jnp.concatenate(parts, axis=1)


VMEM = pl.BlockSpec(memory_space=pltpu.VMEM)
SMEM = pl.BlockSpec(memory_space=pltpu.SMEM)
ANY = pl.BlockSpec(memory_space=pl.ANY)


def call(body, in_specs, out_specs, out_shape, scratch=(), mib=58, flops=1000):
    return pl.pallas_call(
        body,
        in_specs=in_specs,
        out_specs=out_specs,
        out_shape=out_shape,
        scratch_shapes=list(scratch),
        compiler_params=pltpu.CompilerParams(vmem_limit_bytes=mib * MIB),
        cost_estimate=pl.CostEstimate(flops=flops, bytes_accessed=1000, transcendentals=0),
    )


def paired(tokens, expert_ids, combine_weights, out_grad, w_gate_up, w_down):
    count, top = expert_ids.shape
    width = tokens.shape[1]
    scale = 1.0 / math.sqrt(8 * count * top)
    place = lax.axis_index("dp")
    line = lax.axis_index("expert")
    core = place % 2
    spot = jnp.stack([core, place // 2, line]).astype(jnp.int32)
    block = w_gate_up.shape[1]
    full = 8 * PAD
    units = 4 * PAD
    rows = 8 * count
    dma = pltpu.SemaphoreType.DMA

    def swap(bit):
        pairs = [(i, i ^ bit) for i in range(8)]
        return lambda value: lax.ppermute(value, "dp", pairs)

    over_core, over_x, over_y = swap(1), swap(2), swap(4)

    def onward(value):
        return lax.ppermute(value, "expert", [(i, (i + 1) % 4) for i in range(4)])

    def backward(value):
        return lax.ppermute(value, "expert", [(i, (i + 3) % 4) for i in range(4)])

    def array(*shape):
        return jax.ShapeDtypeStruct(shape, BF)

    def held(*shape):
        return pltpu.VMEM(shape, BF)

    def together(*values):
        return lax.optimization_barrier(values)

    x0, g0, own, other, low, high = call(
        prepare_kernel,
        [SMEM] + [VMEM] * 6,
        [VMEM] * 6,
        [array(count, full)] * 2 + [array(PAD, full)] * 2 + [array(LOT, full)] * 2,
    )(spot, tokens.T, out_grad.T, expert_ids.T, combine_weights.T, w_gate_up[0], w_down[0])

    def beside(*values):
        return jnp.concatenate(values, axis=1)

    other, own_x, own_y, x1, fx0 = over_core(other), over_x(own), over_y(own), onward(x0), over_core(x0)
    other = call(join_kernel, [VMEM] * 2, VMEM, array(PAD, full))(other, w_down[0])
    own_x, own_y, x1, other, fx0, g0, low, high = together(own_x, own_y, x1, other, fx0, g0, low, high)
    other_x, other_y, xg2 = over_x(other), over_y(other), onward(beside(x1, g0))
    fx1, fg0 = over_core(x1), over_core(g0)
    other_x, other_y, xg2, fx1, fg0, own_x, low, high = together(other_x, other_y, xg2, fx1, fg0, own_x, low, high)
    own_xy, other_xy, xg3, fxg2 = over_y(own_x), over_x(other_y), onward(xg2), over_core(xg2)
    own_xy, other_xy, xg3, fxg2, low, high = together(own_xy, other_xy, xg3, fxg2, low, high)
    fxg3 = over_core(xg3)
    g3 = onward(xg3[:, full:])
    low_x, high_y, low_y, high_x = over_x(low), over_y(high), over_y(low), over_x(high)

    owns = (own, own_x, own_y, own_xy)
    others = (other, other_x, other_y, other_xy)
    xs = (x0, x1, xg2, xg3, fx0, fx1, fxg2, fxg3)

    hid, up_f, gate_f = call(
        hidden_kernel,
        [SMEM] + [ANY] * 16,
        [ANY] * 3,
        [array(rows, units)] * 3,
        [held(full, full), held(rows, full)] + [held(rows, units)] * 3 + [dma((8,)), dma((8,)), dma((12,))],
        flops=LONG,
    )(spot, *owns, *others, *xs)
    hid, g3, low_x, high_y, low_y, high_x = together(hid, g3, low_x, high_y, low_y, high_x)
    low_xy, high_xy, fg3 = over_y(low_x), over_x(high_y), over_core(g3)
    lows = (low, low_x, low_y, low_xy)
    highs = (high, high_x, high_y, high_xy)
    weights_in = owns + others + lows + highs
    grad, *down_parts = call(
        functools.partial(down_grad_kernel, scale),
        [SMEM] + [ANY] * 9,
        [ANY] * 5,
        [array(rows, full)] + [array(2, HALF, full)] * 4,
        [held(rows, units), held(rows, full), held(units, full), dma((1,)), dma((8,)), dma((4,)), dma((8,))],
        flops=LONG,
    )(spot, hid, g0, xg2, xg3, g3, fg0, fxg2, fxg3, fg3)
    row_shapes = [array(rows // 2, full), array(count, full), array(3 * count, full)]

    def edge_weight(piece):
        tail = lax.dynamic_slice_in_dim(piece, width + line, 5, 1).astype(F32)
        return tail[:, :1] + tail[:, 4:]

    weights = [edge_weight(p) for p in (g0, xg2[:, full:], xg3[:, full:], g3)]

    def slot_sum(own_part, far_part, s, far_at, scaled):
        value = own_part[s * count : (s + 1) * count].astype(F32) + far_part[far_at * count : (far_at + 1) * count].astype(F32)
        return value * weights[s] if scaled else value

    def after(value, moving):
        return (value + moving.astype(F32)).astype(BF)

    def first_step(parts):
        return over_x(parts[0]), over_y(parts[2])

    def passed_on(parts, got):
        def add(a, b):
            return (a[1].astype(F32) + b[1].astype(F32)).astype(BF)

        return add(parts[1], got[0]), add(parts[3], got[1])

    def second_step(away):
        return over_y(away[0]), over_x(away[1])

    def totals(parts, got, last):
        def add(a, b, c):
            return a[0].astype(F32) + b[0].astype(F32) + c.astype(F32)

        return add(parts[1], got[0], last[0]), add(parts[3], got[1], last[1])

    down_got = first_step(down_parts)
    out_own, out_first, out_rest, pre_grad, *gate_parts = call(
        functools.partial(gate_grad_kernel, scale),
        [SMEM] + [ANY] * 28,
        [ANY] * 8,
        row_shapes + [array(rows, full)] + [array(2, PAD, units)] * 4,
        [held(units, full), held(rows, units), held(rows, full), held(rows, units), held(rows, units)]
        + [held(rows, full), held(rows, full), held(rows, full), held(full, units)]
        + [dma((16,)), dma((16,)), dma((8,)), dma((3,)), dma((4,)), dma((8,))],
        flops=LONG,
    )(spot, *weights_in, hid, grad, up_f, gate_f, *xs)
    *down_got, pre_grad, out_first, out_rest, gate_a, gate_b = together(
        *down_got, pre_grad, out_first, out_rest, gate_parts[0], gate_parts[2]
    )
    down_away = passed_on(down_parts, down_got)
    mix3 = slot_sum(out_own, over_core(out_first), 3, 0, True).astype(BF)
    m1 = backward(mix3)
    down_last = second_step(down_away)
    gate_got = over_x(gate_a), over_y(gate_b)
    out_rest = over_core(out_rest)
    in_own, in_first, in_rest, *up_parts = call(
        functools.partial(up_grad_kernel, scale),
        [SMEM] + [ANY] * 17,
        [ANY] * 7,
        row_shapes + [array(2, PAD, units)] * 4,
        [held(full, full), held(rows, full), held(rows, full), held(full, units), held(rows, full)]
        + [dma((8,)), dma((8,)), dma((4,)), dma((3,)), dma((8,))],
        flops=LONG,
    )(spot, *owns, *others, *xs, pre_grad)
    m2 = backward(after(slot_sum(out_own, out_rest, 2, 2, True), m1))
    g1, g2, l1, l2, m2, in_first, in_rest, up_a, up_b = together(
        *gate_got, *down_last, m2, in_first, in_rest, up_parts[0], up_parts[2]
    )
    gate_got, down_last = (g1, g2), (l1, l2)
    m3 = backward(after(slot_sum(out_own, out_rest, 1, 1, True), m2))
    gate_last = second_step(passed_on(gate_parts, gate_got))
    up_got = over_x(up_a), over_y(up_b)
    i1 = backward(slot_sum(in_own, over_core(in_first), 3, 0, False).astype(BF))
    in_rest = over_core(in_rest)

    def finish_rows(value, moving, spread):
        return call(functools.partial(finish_rows_kernel, spread), [VMEM] * 2, VMEM, array(width, count))(value, moving).T

    joined = jnp.concatenate(totals(down_parts, down_got, down_last), axis=0)[:, :width]
    grad_down = jnp.concatenate([joined[:MAIN], joined[164:176], joined[180:]], axis=0)
    u1, u2, l1, l2, m3, i1 = together(*up_got, *gate_last, m3, i1)
    up_got, gate_last = (u1, u2), (l1, l2)
    up_last = second_step(passed_on(up_parts, up_got))
    i2 = backward(after(slot_sum(in_own, in_rest, 2, 2, False), i1))
    mixed_out = finish_rows(slot_sum(out_own, out_rest, 0, 0, True), m3, False)
    i3 = backward(after(slot_sum(in_own, in_rest, 1, 1, False), i2))

    def split(parts, got, last):
        a, b = totals(parts, got, last)
        return jnp.where(core == 0, a, b), over_core(jnp.where(core == 0, b, a).astype(BF))

    gate_keep, gate_far = split(gate_parts, gate_got, gate_last)
    up_keep, up_far = split(up_parts, up_got, up_last)
    token_grad = finish_rows(slot_sum(in_own, in_rest, 0, 0, False), i3, True)
    grad_gate_up = call(
        finish_gate_up_kernel,
        [SMEM] + [VMEM] * 4,
        VMEM,
        jax.ShapeDtypeStruct((block, 2 * width), F32),
    )(spot, gate_keep, gate_far, up_keep, up_far)
    return (mixed_out, token_grad, grad_gate_up[None], grad_down[None])


def solution(mesh):
    placed = (
        P(("dp", "expert"), None),
        P(("dp", "expert"), None),
        P(("dp", "expert"), None),
        P(("dp", "expert"), None),
        P("expert", "dp", None),
        P("expert", "dp", None),
    )
    small = mesh.shape["dp"] == 8 and mesh.shape["expert"] == 4
    return jax.shard_map(
        paired if small else general,
        mesh=mesh,
        in_specs=placed,
        out_specs=(
            P(("dp", "expert"), None),
            P(("dp", "expert"), None),
            P("expert", "dp", None),
            P("expert", "dp", None),
        ),
        check_vma=False,
    )
```

profile of v0, /device:TPU:0, one launch (start us, length us, event | category | flops | bytes accessed | tf_op | source)
XLA Modules:
  0.0 212.2 jit_solution(1399216828819538383)
XLA Ops:
  1.3 4.1 %shard_map.93 = (bf16[128,1536]{1,0:T(8,128)(2,1)}, bf16[128,1536]{1,0:T(8,128)(2,1)}, bf16[192,1536]{1,0:T(8,128)(2,1)}, bf16[192,1536]{1,0:T(8,128)(2,1)}, bf1...) custom-call(s32[3]{0:T(128)} %pad_add_fusion.spot.refs_0_, bf16[1440,128]{1,0:T(8,128)(2,1)} %bitcast.58, ...), custom_call_target="tpu_custom_call" | custom-call | flops 1000 | bytes 1000 | tf_op jit(solution)/shard_map/pallas_call | solution.py:408
  5.8 2.6 %collective-permute-start.1 = (bf16[192,1536]{1,0:T(8,128)(2,1)}, bf16[192,1536]{1,0:T(8,128)(2,1)S(1)}, u32[]{:S(2)}, u32[]{:S(2)}) collective-permute-start(bf16[192,1536]{1,0:T(8,128)(2,1)} %get-tuple-element.83.refs_1_), channel_id=1, source_target_pairs={{0,16},{4,20},{8,24},{12,28},{16,0},{20,4},{24,8},{28,12},{1,17},{... | collective-permute-start | bytes 1769480 | tf_op jit(solution)/shard_map/ppermute | solution.py:389
  14.5 9.1 %collective-permute-done.2.refs_10_.refs_22_ = bf16[128,1536]{1,0:T(8,128)(2,1)S(1)} collective-permute-done((bf16[128,1536]{1,0:T(8,128)(2,1)}, bf16[128,1536]{1,0:T(8,128)(2,1)S(1)}, u32[]{:S(2)}, u32[]{:S(2)}) %collective-permute-start.2) | collective-permute-done | bytes 393248 | tf_op jit(solution)/shard_map/ppermute | solution.py:394
  30.1 10.0 %collective-permute-done.6.refs_7_ = bf16[192,1536]{1,0:T(8,128)(2,1)S(1)} collective-permute-done((bf16[192,1536]{1,0:T(8,128)(2,1)S(1)}, bf16[192,1536]{1,0:T(8,128)(2,1)S(1)}, u32[]{:S(2)}, u32[]{:S(2)}) %collective-permute-start.6) | collective-permute-done | bytes 589856 | tf_op jit(solution)/shard_map/ppermute | solution.py:389
  40.4 4.4 %collective-permute-done.7.refs_11_.refs_3_.refs_23_ = bf16[128,3072]{1,0:T(8,128)(2,1)S(1)} collective-permute-done((bf16[128,3072]{1,0:T(8,128)(2,1)S(1)}, bf16[128,3072]{1,0:T(8,128)(2,1)S(1)}, u32[]{:S(2)}, u32[]{:S(2)}) %collective-permute-start.7) | collective-permute-done | bytes 786464 | tf_op jit(solution)/shard_map/ppermute | solution.py:394
  47.1 13.5 %collective-permute-done.10.refs_4_ = bf16[192,1536]{1,0:T(8,128)(2,1)S(1)} collective-permute-done((bf16[192,1536]{1,0:T(8,128)(2,1)S(1)}, bf16[192,1536]{1,0:T(8,128)(2,1)S(1)}, u32[]{:S(2)}, u32[]{:S(2)}) %collective-permute-start.10) | collective-permute-done | bytes 589856 | tf_op jit(solution)/shard_map/ppermute | solution.py:389
  61.0 5.7 %collective-permute-done.12.refs_12_.refs_4_.refs_24_ = bf16[128,3072]{1,0:T(8,128)(2,1)S(1)} collective-permute-done((bf16[128,3072]{1,0:T(8,128)(2,1)S(1)}, bf16[128,3072]{1,0:T(8,128)(2,1)S(1)}, u32[]{:S(2)}, u32[]{:S(2)}) %collective-permute-start.12) | collective-permute-done | bytes 786464 | tf_op jit(solution)/shard_map/ppermute | solution.py:394
  71.8 11.1 %shard_map.95 = (bf16[1024,768]{1,0:T(8,128)(2,1)}, bf16[1024,768]{1,0:T(8,128)(2,1)}, bf16[1024,768]{1,0:T(8,128)(2,1)}) custom-call(s32[3]{0:T(128)} %pad_add_fusion.spot.refs_0_, bf16[192,1536]{1,0:T(8,128)(2,1)} %get-tuple-element.83.refs_1_, bf16[192,1536]{1,0:T(8,128)(2,1)} %copy-done.22, bf16[192,1536]{1,0:T(8,128)(2,1)} %copy-done.21, ...), custom_call_target="tpu_custom_call" | custom-call | flops 30000001024 | bytes 1000 | tf_op jit(solution)/shard_map/pallas_call | solution.py:434
  87.4 7.5 %shard_map.96 = (bf16[1024,1536]{1,0:T(8,128)(2,1)}, bf16[2,96,1536]{2,1,0:T(8,128)(2,1)}, bf16[2,96,1536]{2,1,0:T(8,128)(2,1)}, bf16[2,96,1536]{2,1,0:T(8,128)(2,1)}, bf16[2,96,1536]{2,1,0:T(8,128)(2,1)}) custom-call(s32[3]{0:T(128)} %pad_add_fusion.spot.refs_0_, bf16[1024,768]{1,0:T(8,128)(2,1)} %get-tuple-element.115.refs_1_.refs_17_, ...), custom_call_target="tpu_custom_call" | custom-call | flops 30000001024 | bytes 1000 | tf_op jit(solution)/shard_map/pallas_call | solution.py:447
  97.8 17.1 %shard_map.97 = (bf16[512,1536]{1,0:T(8,128)(2,1)}, bf16[128,1536]{1,0:T(8,128)(2,1)}, bf16[384,1536]{1,0:T(8,128)(2,1)}, bf16[1024,1536]{1,0:T(8,128)(2,1)}, bf...) custom-call(s32[3]{0:T(128)} %pad_add_fusion.spot.refs_0_, ...), custom_call_target="tpu_custom_call" | custom-call | flops 30000001024 | bytes 1000 | tf_op jit(solution)/shard_map/pallas_call | solution.py:489
  118.9 3.0 %collective-permute-start.31 = (bf16[128,1536]{1,0:T(8,128)(2,1)S(1)}, bf16[128,1536]{1,0:T(8,128)(2,1)S(1)}, u32[]{:S(2)}, u32[]{:S(2)}) collective-permute-start(bf16[128,1536]{1,0:T(8,128)(2,1)S(1)} %multiply_convert_fusion), channel_id=1, source_target_pairs={{0,3},{1,0},{2,1},{3,2},{4,7},{5,4},{6,5},{7,6},{8,11},{9,8},{10,9... | collective-permute-start | bytes 1179656 | tf_op jit(solution)/shard_map/ppermute | solution.py:397
  123.9 6.3 %collective-permute-done.31 = bf16[128,1536]{1,0:T(8,128)(2,1)S(1)} collective-permute-done((bf16[128,1536]{1,0:T(8,128)(2,1)S(1)}, bf16[128,1536]{1,0:T(8,128)(2,1)S(1)}, u32[]{:S(2)}, u32[]{:S(2)}) %collective-permute-start.31) | collective-permute-done | bytes 393248 | tf_op jit(solution)/shard_map/ppermute | solution.py:397
  131.0 4.3 %collective-permute-start.32 = (bf16[128,1536]{1,0:T(8,128)(2,1)S(1)}, bf16[128,1536]{1,0:T(8,128)(2,1)}, u32[]{:S(2)}, u32[]{:S(2)}) collective-permute-start(bf16[128,1536]{1,0:T(8,128)(2,1)S(1)} %add_convert_fusion.4), channel_id=1, source_target_pairs={{0,3},{1,0},{2,1},{3,2},{4,7},{5,4},{6,5},{7,6},{8,11},{9,8},{10,9... | collective-permute-start | bytes 1179656 | tf_op jit(solution)/shard_map/ppermute | solution.py:397
  135.4 14.2 %shard_map.98 = (bf16[512,1536]{1,0:T(8,128)(2,1)}, bf16[128,1536]{1,0:T(8,128)(2,1)}, bf16[384,1536]{1,0:T(8,128)(2,1)}, bf16[2,192,768]{2,1,0:T(8,128)(2,1)}, ...) custom-call(s32[3]{0:T(128)} %pad_add_fusion.spot.refs_0_, ...), custom_call_target="tpu_custom_call" | custom-call | flops 30000001024 | bytes 1000 | tf_op jit(solution)/shard_map/pallas_call | solution.py:508
  156.2 2.2 %add_convert_fusion.3 = (bf16[128,1536]{1,0:T(8,128)(2,1)S(1)}, f32[128,1536]{1,0:T(8,128)}) fusion(bf16[128,1536]{1,0:T(8,128)(2,1)} %collective-permute-done.32, bf16[384,1536]{1,0:T(8,128)(2,1)S(1)} %collective-permute-done.25, f32[128]{0:T(128)S(1)} %fusion.11, bf16[512,1536]{1,0:T(8,128)(2,1)S(1)} %copy-done.1, f32[128]{0:T(128)S(1)} %fusion.14), kind=kLoop, calls=%fused_computation.10 | loop fusion | flops 2162688 | bytes 3146752 | tf_op jit(solution)/shard_map/convert_element_type | solution.py:468
  159.5 2.9 %collective-permute-done.35 = bf16[192,768]{1,0:T(8,128)(2,1)S(1)} collective-permute-done((bf16[192,768]{1,0:T(8,128)(2,1)S(1)}, bf16[192,768]{1,0:T(8,128)(2,1)S(1)}, u32[]{:S(2)}, u32[]{:S(2)}) %collective-permute-start.35) | collective-permute-done | bytes 294944 | tf_op jit(solution)/shard_map/ppermute | solution.py:389
  164.4 6.4 %collective-permute-done.37.got = bf16[128,1536]{1,0:T(8,128)(2,1)S(1)} collective-permute-done((bf16[128,1536]{1,0:T(8,128)(2,1)S(1)}, bf16[128,1536]{1,0:T(8,128)(2,1)S(1)}, u32[]{:S(2)}, u32[]{:S(2)}) %collective-permute-start.37) | collective-permute-done | bytes 393248 | tf_op jit(solution)/shard_map/ppermute | solution.py:397
  170.8 2.2 %collective-permute-done.34 = bf16[2,192,768]{2,1,0:T(8,128)(2,1)S(1)} collective-permute-done((bf16[2,192,768]{2,1,0:T(8,128)(2,1)S(1)}, bf16[2,192,768]{2,1,0:T(8,128)(2,1)S(1)}, u32[]{:S(2)}, u32[]{:S(2)}) %collective-permute-start.34) | collective-permute-done | bytes 589856 | tf_op jit(solution)/shard_map/ppermute | solution.py:389
  173.0 5.5 %collective-permute-done.39 = bf16[128,1536]{1,0:T(8,128)(2,1)S(1)} collective-permute-done((bf16[128,1536]{1,0:T(8,128)(2,1)S(1)}, bf16[128,1536]{1,0:T(8,128)(2,1)S(1)}, u32[]{:S(2)}, u32[]{:S(2)}) %collective-permute-start.39) | collective-permute-done | bytes 393248 | tf_op jit(solution)/shard_map/ppermute | solution.py:397
  181.4 2.4 %collective-permute-start.41 = (bf16[128,1536]{1,0:T(8,128)(2,1)S(1)}, bf16[128,1536]{1,0:T(8,128)(2,1)S(1)}, u32[]{:S(2)}, u32[]{:S(2)}) collective-permute-start(bf16[128,1536]{1,0:T(8,128)(2,1)S(1)} %add_convert_fusion.1), channel_id=1, source_target_pairs={{0,3},{1,0},{2,1},{3,2},{4,7},{5,4},{6,5},{7,6},{8,11},{9,8},{10,9... | collective-permute-start | bytes 1179656 | tf_op jit(solution)/shard_map/ppermute | solution.py:397
  191.2 3.4 %collective-permute-start.42 = (bf16[128,1536]{1,0:T(8,128)(2,1)S(1)}, bf16[128,1536]{1,0:T(8,128)(2,1)S(1)}, u32[]{:S(2)}, u32[]{:S(2)}) collective-permute-start(bf16[128,1536]{1,0:T(8,128)(2,1)S(1)} %get-tuple-element.174), channel_id=1, source_target_pairs={{0,3},{1,0},{2,1},{3,2},{4,7},{5,4},{6,5},{7,6},{8,11},{9,8},{10,9... | collective-permute-start | bytes 1179656 | tf_op jit(solution)/shard_map/ppermute | solution.py:397
  196.9 2.2 %shard_map.99 = bf16[1440,128]{1,0:T(8,128)(2,1)} custom-call(f32[128,1536]{1,0:T(8,128)} %get-tuple-element.177.keep, bf16[128,1536]{1,0:T(8,128)(2,1)} %copy-done.12), custom_call_target="tpu_custom_call" | custom-call | flops 1000 | bytes 1000 | tf_op jit(solution)/shard_map/pallas_call | solution.py:529
  199.9 4.3 %shard_map.101 = f32[180,2880]{1,0:T(8,128)} custom-call(s32[3]{0:T(128)} %pad_add_fusion.spot.refs_0_, f32[192,768]{1,0:T(8,128)} %get-tuple-element.173.gate_keep, bf16[192,768]{1,0:T(8,128)(2,1)} %copy-done.14, f32[192,768]{1,0:T(8,128)} %get-tuple-element.171.up_keep, bf16[192,768]{1,0:T(8,128)(2,1)} %copy-done.15), custom_call_target="tpu_custom_call" | custom-call | flops 1000 | bytes 1000 | tf_op jit(solution)/shard_map/pallas_call | solution.py:547
  204.2 5.1 %copy.12 = f32[1,180,2880]{2,0,1:T(1,128)} copy(f32[1,180,2880]{2,1,0:T(8,128)} %bitcast.54) | data formatting | bytes 4147200
  (194 shorter events, 61.5 us)
Async XLA Ops:
  5.8 17.7 %collective-permute-start.1 = (bf16[192,1536]{1,0:T(8,128)(2,1)}, bf16[192,1536]{1,0:T(8,128)(2,1)S(1)}, u32[]{:S(2)}, u32[]{:S(2)}) collective-permute-start(bf16[192,1536]{1,0:T(8,128)(2,1)} %get-tuple-element.83.refs_1_), channel_id=1, source_target_pairs={{0,16},{4,20},{8,24},{12,28},{16,0},{20,4},{24,8},{28,12},{1,17},{... | collective-permute-start | bytes 1769480 | tf_op jit(solution)/shard_map/ppermute | solution.py:389
  8.4 15.6 %collective-permute-start = (bf16[192,1536]{1,0:T(8,128)(2,1)}, bf16[192,1536]{1,0:T(8,128)(2,1)S(1)}, u32[]{:S(2)}, u32[]{:S(2)}) collective-permute-start(bf16[192,1536]{1,0:T(8,128)(2,1)} %get-tuple-element.83.refs_1_), channel_id=1, source_target_pairs={{0,8},{4,12},{8,0},{12,4},{16,24},{20,28},{24,16},{28,20},{1,9},{5... | collective-permute-start | bytes 1769480 | tf_op jit(solution)/shard_map/ppermute | solution.py:389
  24.1 20.7 %collective-permute-start.7 = (bf16[128,3072]{1,0:T(8,128)(2,1)S(1)}, bf16[128,3072]{1,0:T(8,128)(2,1)S(1)}, u32[]{:S(2)}, u32[]{:S(2)}) collective-permute-start(bf16[128,3072]{1,0:T(8,128)(2,1)S(1)} %pad_maximum_fusion), channel_id=1, source_target_pairs={{0,1},{1,2},{2,3},{3,0},{4,5},{5,6},{6,7},{7,4},{8,9},{9,10},{10,1... | collective-permute-start | bytes 2359304 | tf_op jit(solution)/shard_map/ppermute | solution.py:394
  25.8 14.3 %collective-permute-start.6 = (bf16[192,1536]{1,0:T(8,128)(2,1)S(1)}, bf16[192,1536]{1,0:T(8,128)(2,1)S(1)}, u32[]{:S(2)}, u32[]{:S(2)}) collective-permute-start(bf16[192,1536]{1,0:T(8,128)(2,1)S(1)} %copy-done.4), channel_id=1, source_target_pairs={{0,16},{4,20},{8,24},{12,28},{16,0},{20,4},{24,8},{28,12},{1,17},{... | collective-permute-start | bytes 1769480 | tf_op jit(solution)/shard_map/ppermute | solution.py:389
  26.3 14.1 %collective-permute-start.5 = (bf16[192,1536]{1,0:T(8,128)(2,1)S(1)}, bf16[192,1536]{1,0:T(8,128)(2,1)S(1)}, u32[]{:S(2)}, u32[]{:S(2)}) collective-permute-start(bf16[192,1536]{1,0:T(8,128)(2,1)S(1)} %copy-done.4), channel_id=1, source_target_pairs={{0,8},{4,12},{8,0},{12,4},{16,24},{20,28},{24,16},{28,20},{1,9},{5... | collective-permute-start | bytes 1769480 | tf_op jit(solution)/shard_map/ppermute | solution.py:389
  44.9 16.1 %collective-permute-start.13 = (bf16[128,3072]{1,0:T(8,128)(2,1)S(1)}, bf16[128,3072]{1,0:T(8,128)(2,1)S(1)}, u32[]{:S(2)}, u32[]{:S(2)}) collective-permute-start(bf16[128,3072]{1,0:T(8,128)(2,1)S(1)} %collective-permute-done.7.refs_11_.refs_3_.refs_23_), channel_id=1, source_target_pairs={{0,4},{4,0},{8,12},{12,8},{16,20},{20,16},{24,28},{28,24},{1,5},{5... | collective-permute-start | bytes 2359304 | tf_op jit(solution)/shard_map/ppermute | solution.py:389
  44.9 21.7 %collective-permute-start.12 = (bf16[128,3072]{1,0:T(8,128)(2,1)S(1)}, bf16[128,3072]{1,0:T(8,128)(2,1)S(1)}, u32[]{:S(2)}, u32[]{:S(2)}) collective-permute-start(bf16[128,3072]{1,0:T(8,128)(2,1)S(1)} %collective-permute-done.7.refs_11_.refs_3_.refs_23_), channel_id=1, source_target_pairs={{0,1},{1,2},{2,3},{3,0},{4,5},{5,6},{6,7},{7,4},{8,9},{9,10},{10,1... | collective-permute-start | bytes 2359304 | tf_op jit(solution)/shard_map/ppermute | solution.py:394
  44.9 15.7 %collective-permute-start.10 = (bf16[192,1536]{1,0:T(8,128)(2,1)S(1)}, bf16[192,1536]{1,0:T(8,128)(2,1)S(1)}, u32[]{:S(2)}, u32[]{:S(2)}) collective-permute-start(bf16[192,1536]{1,0:T(8,128)(2,1)S(1)} %collective-permute-done.refs_2_), channel_id=1, source_target_pairs={{0,16},{4,20},{8,24},{12,28},{16,0},{20,4},{24,8},{28,12},{1,17},{... | collective-permute-start | bytes 1769480 | tf_op jit(solution)/shard_map/ppermute | solution.py:389
  45.6 15.3 %collective-permute-start.11 = (bf16[192,1536]{1,0:T(8,128)(2,1)S(1)}, bf16[192,1536]{1,0:T(8,128)(2,1)S(1)}, u32[]{:S(2)}, u32[]{:S(2)}) collective-permute-start(bf16[192,1536]{1,0:T(8,128)(2,1)S(1)} %collective-permute-done.6.refs_7_), channel_id=1, source_target_pairs={{0,8},{4,12},{8,0},{12,4},{16,24},{20,28},{24,16},{28,20},{1,9},{5... | collective-permute-start | bytes 1769480 | tf_op jit(solution)/shard_map/ppermute | solution.py:389
  67.4 15.5 %collective-permute-start.18 = (bf16[80,1536]{1,0:T(8,128)(2,1)S(1)}, bf16[80,1536]{1,0:T(8,128)(2,1)S(1)}, u32[]{:S(2)}, u32[]{:S(2)}) collective-permute-start(bf16[80,1536]{1,0:T(8,128)(2,1)S(1)} %copy-done.34), channel_id=1, source_target_pairs={{0,16},{4,20},{8,24},{12,28},{16,0},{20,4},{24,8},{28,12},{1,17},{... | collective-permute-start | bytes 737288 | tf_op jit(solution)/shard_map/ppermute | solution.py:389
  68.0 14.9 %collective-permute-start.16 = (bf16[80,1536]{1,0:T(8,128)(2,1)S(1)}, bf16[80,1536]{1,0:T(8,128)(2,1)S(1)}, u32[]{:S(2)}, u32[]{:S(2)}) collective-permute-start(bf16[80,1536]{1,0:T(8,128)(2,1)S(1)} %copy-done.34), channel_id=1, source_target_pairs={{0,8},{4,12},{8,0},{12,4},{16,24},{20,28},{24,16},{28,20},{1,9},{5... | collective-permute-start | bytes 737288 | tf_op jit(solution)/shard_map/ppermute | solution.py:389
  95.0 19.9 %collective-permute-start.23 = (bf16[2,96,1536]{2,1,0:T(8,128)(2,1)}, bf16[2,96,1536]{2,1,0:T(8,128)(2,1)S(1)}, u32[]{:S(2)}, u32[]{:S(2)}) collective-permute-start(bf16[2,96,1536]{2,1,0:T(8,128)(2,1)} %get-tuple-element.122), channel_id=1, source_target_pairs={{0,8},{4,12},{8,0},{12,4},{16,24},{20,28},{24,16},{28,20},{1,9},{5... | collective-permute-start | bytes 1769480 | tf_op jit(solution)/shard_map/ppermute | solution.py:389
  95.6 19.3 %collective-permute-start.24 = (bf16[2,96,1536]{2,1,0:T(8,128)(2,1)}, bf16[2,96,1536]{2,1,0:T(8,128)(2,1)S(1)}, u32[]{:S(2)}, u32[]{:S(2)}) collective-permute-start(bf16[2,96,1536]{2,1,0:T(8,128)(2,1)} %get-tuple-element.123), channel_id=1, source_target_pairs={{0,16},{4,20},{8,24},{12,28},{16,0},{20,4},{24,8},{28,12},{1,17},{... | collective-permute-start | bytes 1769480 | tf_op jit(solution)/shard_map/ppermute | solution.py:389
  114.9 15.9 %collective-permute-start.25 = (bf16[384,1536]{1,0:T(8,128)(2,1)}, bf16[384,1536]{1,0:T(8,128)(2,1)S(1)}, u32[]{:S(2)}, u32[]{:S(2)}) collective-permute-start(bf16[384,1536]{1,0:T(8,128)(2,1)} %get-tuple-element.129), channel_id=1, source_target_pairs={{0,4},{4,0},{8,12},{12,8},{16,20},{20,16},{24,28},{28,24},{1,5},{5... | collective-permute-start | bytes 3538952 | tf_op jit(solution)/shard_map/ppermute | solution.py:389
  116.2 33.3 %collective-permute-start.29 = (bf16[96,1536]{1,0:T(8,128)(2,1)}, bf16[96,1536]{1,0:T(8,128)(2,1)}, u32[]{:S(2)}, u32[]{:S(2)}) collective-permute-start(bf16[96,1536]{1,0:T(8,128)(2,1)} %fusion.6), channel_id=1, source_target_pairs={{0,8},{4,12},{8,0},{12,4},{16,24},{20,28},{24,16},{28,20},{1,9},{5... | collective-permute-start | bytes 884744 | tf_op jit(solution)/shard_map/ppermute | solution.py:389
  122.7 26.9 %collective-permute-start.28 = (bf16[96,1536]{1,0:T(8,128)(2,1)}, bf16[96,1536]{1,0:T(8,128)(2,1)}, u32[]{:S(2)}, u32[]{:S(2)}) collective-permute-start(bf16[96,1536]{1,0:T(8,128)(2,1)} %fusion.5), channel_id=1, source_target_pairs={{0,16},{4,20},{8,24},{12,28},{16,0},{20,4},{24,8},{28,12},{1,17},{... | collective-permute-start | bytes 884744 | tf_op jit(solution)/shard_map/ppermute | solution.py:389
  123.3 26.3 %collective-permute-start.26 = (bf16[2,192,768]{2,1,0:T(8,128)(2,1)}, bf16[2,192,768]{2,1,0:T(8,128)(2,1)}, u32[]{:S(2)}, u32[]{:S(2)}) collective-permute-start(bf16[2,192,768]{2,1,0:T(8,128)(2,1)} %get-tuple-element.130), channel_id=1, source_target_pairs={{0,8},{4,12},{8,0},{12,4},{16,24},{20,28},{24,16},{28,20},{1,9},{5... | collective-permute-start | bytes 1769480 | tf_op jit(solution)/shard_map/ppermute | solution.py:389
  130.2 19.4 %collective-permute-start.27 = (bf16[2,192,768]{2,1,0:T(8,128)(2,1)}, bf16[2,192,768]{2,1,0:T(8,128)(2,1)}, u32[]{:S(2)}, u32[]{:S(2)}) collective-permute-start(bf16[2,192,768]{2,1,0:T(8,128)(2,1)} %get-tuple-element.131), channel_id=1, source_target_pairs={{0,16},{4,20},{8,24},{12,28},{16,0},{20,4},{24,8},{28,12},{1,17},{... | collective-permute-start | bytes 1769480 | tf_op jit(solution)/shard_map/ppermute | solution.py:389
  131.0 18.6 %collective-permute-start.32 = (bf16[128,1536]{1,0:T(8,128)(2,1)S(1)}, bf16[128,1536]{1,0:T(8,128)(2,1)}, u32[]{:S(2)}, u32[]{:S(2)}) collective-permute-start(bf16[128,1536]{1,0:T(8,128)(2,1)S(1)} %add_convert_fusion.4), channel_id=1, source_target_pairs={{0,3},{1,0},{2,1},{3,2},{4,7},{5,4},{6,5},{7,6},{8,11},{9,8},{10,9... | collective-permute-start | bytes 1179656 | tf_op jit(solution)/shard_map/ppermute | solution.py:397
  154.4 16.4 %collective-permute-start.33 = (bf16[2,192,768]{2,1,0:T(8,128)(2,1)S(1)}, bf16[2,192,768]{2,1,0:T(8,128)(2,1)S(1)}, u32[]{:S(2)}, u32[]{:S(2)}) collective-permute-start(bf16[2,192,768]{2,1,0:T(8,128)(2,1)S(1)} %copy-done.28), channel_id=1, source_target_pairs={{0,8},{4,12},{8,0},{12,4},{16,24},{20,28},{24,16},{28,20},{1,9},{5... | collective-permute-start | bytes 1769480 | tf_op jit(solution)/shard_map/ppermute | solution.py:389
  155.6 17.5 %collective-permute-start.34 = (bf16[2,192,768]{2,1,0:T(8,128)(2,1)S(1)}, bf16[2,192,768]{2,1,0:T(8,128)(2,1)S(1)}, u32[]{:S(2)}, u32[]{:S(2)}) collective-permute-start(bf16[2,192,768]{2,1,0:T(8,128)(2,1)S(1)} %copy-done.27), channel_id=1, source_target_pairs={{0,16},{4,20},{8,24},{12,28},{16,0},{20,4},{24,8},{28,12},{1,17},{... | collective-permute-start | bytes 1769480 | tf_op jit(solution)/shard_map/ppermute | solution.py:389
  158.4 22.8 %collective-permute-start.40 = (bf16[384,1536]{1,0:T(8,128)(2,1)S(1)}, bf16[384,1536]{1,0:T(8,128)(2,1)S(1)}, u32[]{:S(2)}, u32[]{:S(2)}) collective-permute-start(bf16[384,1536]{1,0:T(8,128)(2,1)S(1)} %copy-done.19), channel_id=1, source_target_pairs={{0,4},{4,0},{8,12},{12,8},{16,20},{20,16},{24,28},{28,24},{1,5},{5... | collective-permute-start | bytes 3538952 | tf_op jit(solution)/shard_map/ppermute | solution.py:389
  162.4 16.1 %collective-permute-start.39 = (bf16[128,1536]{1,0:T(8,128)(2,1)S(1)}, bf16[128,1536]{1,0:T(8,128)(2,1)S(1)}, u32[]{:S(2)}, u32[]{:S(2)}) collective-permute-start(bf16[128,1536]{1,0:T(8,128)(2,1)S(1)} %add_convert_fusion.2), channel_id=1, source_target_pairs={{0,3},{1,0},{2,1},{3,2},{4,7},{5,4},{6,5},{7,6},{8,11},{9,8},{10,9... | collective-permute-start | bytes 1179656 | tf_op jit(solution)/shard_map/ppermute | solution.py:397
  191.2 18.1 %collective-permute-start.42 = (bf16[128,1536]{1,0:T(8,128)(2,1)S(1)}, bf16[128,1536]{1,0:T(8,128)(2,1)S(1)}, u32[]{:S(2)}, u32[]{:S(2)}) collective-permute-start(bf16[128,1536]{1,0:T(8,128)(2,1)S(1)} %get-tuple-element.174), channel_id=1, source_target_pairs={{0,3},{1,0},{2,1},{3,2},{4,7},{5,4},{6,5},{7,6},{8,11},{9,8},{10,9... | collective-permute-start | bytes 1179656 | tf_op jit(solution)/shard_map/ppermute | solution.py:397
  (65 other events, 715.6 us)
where the time goes:
time: 213 us; the launch traced here: 212 us
  waiting for transfers between devices  73.3 us (34%)
  Pallas kernels  64.6 us (30%)
  starting transfers between devices  46.4 us (22%)
  other arithmetic  15.2 us (7%)
  local copies, waits for them, and re-layouts  11.4 us (5%)
    ppermute x37, waiting for transfers between devices, swap(): return lambda value: lax.ppermute(value, 'dp', pairs)  33.3 us
    ppermute x37, starting transfers between devices, swap(): return lambda value: lax.ppermute(value, 'dp', pairs)  28.3 us
    ppermute x4, waiting for transfers between devices, onward(): return lax.ppermute(value, 'expert', [(i, (i + 1) % 4) for i in range(4)])  20.1 us
    ppermute x6, waiting for transfers between devices, backward(): return lax.ppermute(value, 'expert', [(i, (i + 3) % 4) for i in range(4)])  19.9 us
    pallas_call x1, Pallas kernels, paired(): call(functools.partial(gate_grad_kernel, scale), [SMEM] + [ANY] * 28, [AN...  17.1 us
    ppermute x6, starting transfers between devices, backward(): return lax.ppermute(value, 'expert', [(i, (i + 3) % 4) for i in range(4)])  14.6 us
    pallas_call x1, Pallas kernels, paired(): call(functools.partial(up_grad_kernel, scale), [SMEM] + [ANY] * 17, [ANY]...  14.2 us
    unnamed x86, local copies, waits for them, and re-layouts  11.3 us
  transfers between devices with their start and end apart: 47, of which 21 were waited for; matrix products, arithmetic and copies ran while one was open for 10% of the time, Pallas kernels for 28%

commit v1 on v0

v1 whole, which is shorter than its diff:
```python
import functools
import math

import jax
import jax.numpy as jnp
from jax import lax
from jax.experimental import pallas as pl
from jax.experimental.pallas import tpu as pltpu
from jax.sharding import PartitionSpec as P

GLU_ALPHA = 1.702
BF = jnp.bfloat16
F32 = jnp.float32


def route_matrix(expert_ids, combine_weights, experts):
    hit = expert_ids[:, :, None] == jnp.arange(experts, dtype=jnp.int32)[None, None, :]
    return jnp.sum(jnp.where(hit, combine_weights[:, :, None], 0.0), axis=1)


def dense_forward(rows, weight_gu):
    half = weight_gu.shape[1] // 2
    pre = jnp.dot(rows, weight_gu, preferred_element_type=F32)
    gate, up = pre[:, :half], pre[:, half:]
    sig = jax.nn.sigmoid(GLU_ALPHA * gate)
    glu = gate * sig
    hidden = ((up + 1.0) * glu).astype(BF)
    gate_factor = (up + 1.0) * (sig + GLU_ALPHA * gate * sig * (1.0 - sig))
    return hidden, glu, gate_factor


def contract(left, right, dims):
    return lax.dot_general(left, right, ((dims[:1], dims[1:]), ((), ())), preferred_element_type=F32)


def general(tokens, expert_ids, combine_weights, out_grad, w_gate_up, w_down):
    experts = lax.axis_size("expert")
    replicas = lax.axis_size("dp")
    count, top = expert_ids.shape
    scale = 1.0 / math.sqrt(replicas * count * top)
    me = lax.axis_index("expert")
    table = route_matrix(expert_ids, combine_weights, experts)
    rows = lax.all_gather(tokens, "expert", axis=0, tiled=True)
    grads = lax.all_gather(out_grad, "expert", axis=0, tiled=True)
    table = lax.all_gather(table, "expert", axis=0, tiled=True)
    weight = lax.dynamic_slice_in_dim(table, me, 1, 1)
    row_grad = (weight * grads.astype(F32)).astype(BF)
    weight_gu = lax.all_gather(w_gate_up[0], "dp", axis=0, tiled=True)
    weight_down = lax.all_gather(w_down[0], "dp", axis=0, tiled=True)
    hidden, glu, gate_factor = dense_forward(rows, weight_gu)
    expert_out = jnp.dot(hidden, weight_down, preferred_element_type=F32).astype(BF)
    mixed = (weight * expert_out.astype(F32)).astype(BF)
    hidden_grad = contract(row_grad, weight_down, (1, 1))
    pre_grad = jnp.concatenate([hidden_grad * gate_factor, hidden_grad * glu], axis=1).astype(BF)
    input_grad = contract(pre_grad, weight_gu, (1, 1)).astype(BF)
    part_gu = (contract(rows, pre_grad, (0, 0)) * scale).astype(BF)
    part_down = (contract(hidden, row_grad, (0, 0)) * scale).astype(BF)

    def scatter(value, axis):
        return lax.psum_scatter(value, axis, scatter_dimension=0, tiled=True)

    return (
        scatter(mixed, "expert"),
        scatter(input_grad, "expert"),
        scatter(part_gu, "dp").astype(F32)[None],
        scatter(part_down, "dp").astype(F32)[None],
    )


PAD = 192
HALF = 96
MAIN = 156
LOT = 80
MIB = 1024 * 1024
LONG = 30_000_000_000


def zeros(shape, dtype=F32):
    return jnp.zeros(shape, dtype)


def prepare_kernel(spot, tokens_t, grads_t, ids_t, weights_t, w_gu, w_down, packed, own, other, high):
    core = spot[0]
    width, count = tokens_t.shape
    block = w_gu.shape[0]
    blocks = width // block
    gap = PAD - block
    full = blocks * PAD

    x = tokens_t[...].astype(F32)
    spread = []
    for i in range(blocks):
        spread += [x[i * block : (i + 1) * block], zeros((gap, count))]
    packed[:, :full] = jnp.concatenate(spread, axis=0).T.astype(BF)

    hit = [ids_t[...] == e for e in range(4)]
    table = jnp.concatenate(
        [jnp.sum(jnp.where(h, weights_t[...], 0.0), axis=0, keepdims=True) for h in hit], axis=0
    )
    coarse = table.astype(BF).astype(F32)
    rows = [grads_t[...].astype(F32), coarse, table - coarse, zeros((full - width - 8, count))]
    packed[:, full:] = jnp.concatenate(rows, axis=0).T.astype(BF)

    w = w_gu[...]
    lot = block - MAIN
    edge = zeros((block, lot // 3), BF)
    slim = zeros((block, lot // 6), BF)

    def half(parity):
        parts = []
        for j in range(blocks):
            at = (2 * j + parity) * block
            parts += [w[:, at : at + MAIN], edge, w[:, at + MAIN : at + MAIN + gap], slim, w[:, at + MAIN + gap : at + block]]
        return jnp.concatenate(parts, axis=1)

    even, odd = half(0), half(1)
    down = jnp.concatenate([w_down[...], zeros((block, full - width), BF)], axis=1)
    own[:block, :] = jnp.where(core == 0, even, odd)
    own[block:PAD, :] = down[MAIN : MAIN + gap]
    own[PAD:, :] = down[:LOT]
    other[...] = jnp.concatenate([jnp.where(core == 0, odd, even), zeros((gap, full), BF)], axis=0)
    high[...] = jnp.concatenate([down[LOT:MAIN], zeros((2 * LOT - MAIN, full), BF)], axis=0)


def join_kernel(other, high, w_down, out):
    block = w_down.shape[0]
    gap = PAD - block
    out[:PAD, :] = other[...]
    side = zeros((gap, out.shape[1] - w_down.shape[1]), BF)
    out[block:PAD, :] = jnp.concatenate([w_down[block - gap :, :], side], axis=1)
    out[PAD:, :] = high[...]


def start_all(copies):
    for c in copies:
        c.start()
    return copies


def wait_all(copies):
    for c in copies:
        c.wait()


def gate_up_copies(spot, owns, others, w_gu, sems):
    core, chip = spot[0], spot[1]
    copies = []
    for k in range(4):
        j = jnp.bitwise_xor(chip, k)
        for n, (ref, which) in enumerate(((owns[k], core), (others[k], 1 - core))):
            row = pl.multiple_of((2 * j + which) * PAD, PAD)
            copies.append(pltpu.make_async_copy(ref.at[pl.ds(0, PAD)], w_gu.at[pl.ds(row, PAD)], sems.at[2 * k + n]))
    return copies


def down_copies(spot, owns, others, w_down, sems):
    chip = spot[1]
    copies = []
    for k in range(4):
        base = jnp.bitwise_xor(chip, k) * PAD
        parts = (
            (owns[k].at[pl.ds(PAD, LOT)], 0, LOT),
            (others[k].at[pl.ds(PAD, LOT)], LOT, LOT),
            (owns[k].at[pl.ds(PAD - 16, 16)], 2 * LOT, 16),
            (others[k].at[pl.ds(PAD - 16, 16)], 2 * LOT + 16, 16),
        )
        for ref, at, size in parts:
            row = pl.multiple_of(base + at, 16)
            copies.append(pltpu.make_async_copy(ref, w_down.at[pl.ds(row, size)], sems.at[len(copies)]))
    return copies


def row_copies(pieces, starts, scratch, sems):
    count, wide = pieces[0].shape[0], scratch.shape[1]
    return [
        pltpu.make_async_copy(p.at[:, pl.ds(start, wide)], scratch.at[pl.ds(n * count, count)], sems.at[n])
        for n, (p, start) in enumerate(zip(pieces, starts))
    ]


def chunk_copies(source, target, step, sems, base=0):
    return [
        pltpu.make_async_copy(source.at[pl.ds(m, step)], target.at[pl.ds(m, step)], sems.at[base + m // step])
        for m in range(0, source.shape[0], step)
    ]


STEP = 256
X_AT = (0,) * 8
G_AT = (8 * PAD,) * 8


def scatter_copies(chip, part, stride, a_at, b_at, send_a, keep_a, send_b, keep_b, sems, first=0):
    size = send_a.shape[1]
    copies = []
    plan_a = ((1, send_a, first), (3, send_a, first + 1), (0, keep_a, 0), (2, keep_a, 1))
    plan_b = ((2, send_b, first), (3, send_b, first + 1), (0, keep_b, 0), (1, keep_b, 1))
    for at, plan in ((a_at, plan_a), (b_at, plan_b)):
        for rel, ref, slot in plan:
            row = jnp.bitwise_xor(chip, rel) * (stride * PAD) + at
            source = part.at[pl.ds(pl.multiple_of(row, HALF), size)]
            copies.append(pltpu.make_async_copy(source, ref.at[slot], sems.at[len(copies)]))
    return copies


def forward_kernel(scale, *refs):
    spot, owns, others, pieces = refs[0], refs[1:5], refs[5:9], refs[9:17]
    up_out, gate_out, grad_out, out_own, out_first, out_rest, *parts = refs[17:27]
    w_gu, w_down, x, g, hid, up_f, gate_f, wide, out, part = refs[27:37]
    w_sems, down_sems, x_sems, g_sems, out_sems, row_sems, part_sems = refs[37:]
    line, chip = spot[2], spot[1]
    gu = start_all(gate_up_copies(spot, owns, others, w_gu, w_sems))
    xs = row_copies(pieces, X_AT, x, x_sems)
    gs = row_copies(pieces, G_AT, g, g_sems)
    per = STEP // pieces[0].shape[0]
    start_all(xs[:per])
    wait_all(gu)
    start_all(xs[per:])
    start_all(gs)
    down = start_all(down_copies(spot, owns, others, w_down, down_sems))
    half = w_gu.shape[1] // 2
    full = g.shape[1]
    lane = lax.broadcasted_iota(jnp.int32, (STEP, 128), 1)
    picked = (lane == 32 + line) | (lane == 36 + line)
    outs = [
        chunk_copies(a, b, STEP, out_sems, base) for a, b, base in ((up_f, up_out, 0), (gate_f, gate_out, 4), (g, grad_out, 8))
    ]
    for n in range(x.shape[0] // STEP):
        at = pl.ds(n * STEP, STEP)
        wait_all(xs[n * per : (n + 1) * per])
        pre = jnp.dot(x[at, :], w_gu[...], preferred_element_type=F32)
        gate, up = pre[:, :half], pre[:, half:] + 1.0
        sig = jax.nn.sigmoid(GLU_ALPHA * gate)
        glu = gate * sig
        hid[at, :] = (up * glu).astype(BF)
        up_f[at, :] = glu.astype(BF)
        gate_f[at, :] = (up * (sig + GLU_ALPHA * glu * (1.0 - sig))).astype(BF)
        wait_all(gs[n * per : (n + 1) * per])
        edge = g[at, pl.ds(full - 128, 128)].astype(F32)
        weight = jnp.sum(jnp.where(picked, edge, 0.0), axis=1, keepdims=True)
        g[at, :] = (weight * g[at, :].astype(F32)).astype(BF)
        wide[at, :] = jnp.broadcast_to(weight, (STEP, 128))
        for group in outs:
            group[n].start()
    for m in range(0, part.shape[0], STEP):
        at = pl.ds(m, STEP)
        part[at, :] = (contract(hid[:, at], g[...], (0, 0)) * scale).astype(BF)
    sent = start_all(scatter_copies(chip, part, 1, 0, HALF, *parts, part_sems))
    wait_all(down)
    rows = row_outs(out, out_own, out_first, out_rest, row_sems)
    for n in (3, 2, 1, 0):
        at = pl.ds(n * STEP, STEP)
        part_out = jnp.dot(hid[at, :], w_down[...], preferred_element_type=F32)
        out[at, :] = (part_out * wide[at, :1]).astype(BF)
    start_all(rows)
    for group in outs:
        wait_all(group)
    wait_all(sent)
    wait_all(rows)


def row_outs(out, own, first, rest, sems):
    last = out.shape[0] // 8
    return [
        pltpu.make_async_copy(out.at[pl.ds(7 * last, last)], first, sems.at[0]),
        pltpu.make_async_copy(out.at[pl.ds(4 * last, 3 * last)], rest, sems.at[1]),
        pltpu.make_async_copy(out.at[pl.ds(0, 4 * last)], own, sems.at[2]),
    ]


def gate_grad_kernel(scale, *refs):
    spot, owns, others = refs[0], refs[1:5], refs[5:9]
    grad_in, up_in, gate_in, pieces = refs[9], refs[10], refs[11], refs[12:20]
    pre_out, *parts = refs[20:25]
    w_down, g, up_f, gate_f, pre_grad, x, part, w_sems, in_sems, x_sems, out_sems, part_sems = refs[25:]
    down = start_all(down_copies(spot, owns, others, w_down, w_sems))
    loads = [
        chunk_copies(a, b, STEP, in_sems, base) for a, b, base in ((grad_in, g, 0), (up_in, up_f, 4), (gate_in, gate_f, 8))
    ]
    xs = row_copies(pieces, X_AT, x, x_sems)
    groups = list(zip(*loads))
    start_all(groups[0])
    wait_all(down)
    for group in groups[1:]:
        start_all(group)
    half = w_down.shape[0]
    pres = chunk_copies(pre_grad, pre_out, STEP, out_sems)
    for n, group in enumerate(groups):
        at = pl.ds(n * STEP, STEP)
        wait_all(group)
        if n == 1:
            start_all(xs)
        hidden_grad = contract(g[at, :], w_down[...], (1, 1))
        pre_grad[at, :half] = (hidden_grad * gate_f[at, :].astype(F32)).astype(BF)
        pre_grad[at, half:] = (hidden_grad * up_f[at, :].astype(F32)).astype(BF)
        pres[n].start()
    wait_all(xs)
    for m in range(0, part.shape[0], 2 * PAD):
        at = pl.ds(m, 2 * PAD)
        part[at, :] = (contract(x[:, at], pre_grad[:, :half], (0, 0)) * scale).astype(BF)
    outs = start_all(scatter_copies(spot[1], part, 2, 0, PAD, *parts, part_sems))
    wait_all(pres)
    wait_all(outs)


def up_grad_kernel(scale, *refs):
    spot, owns, others, pieces, pre_in = refs[0], refs[1:5], refs[5:9], refs[9:17], refs[17]
    in_own, in_first, in_rest, *parts = refs[18:25]
    w_gu, x, pre_grad, part, out, w_sems, x_sems, in_sems, out_sems, part_sems = refs[25:]
    loads = start_all(chunk_copies(pre_in, pre_grad, STEP, in_sems))
    xs = start_all(row_copies(pieces, X_AT, x, x_sems))
    wait_all(loads)
    wait_all(xs)
    gu = start_all(gate_up_copies(spot, owns, others, w_gu, w_sems))
    half = part.shape[1]
    for m in range(0, part.shape[0], 2 * PAD):
        at = pl.ds(m, 2 * PAD)
        part[at, :] = (contract(x[:, at], pre_grad[:, half:], (0, 0)) * scale).astype(BF)
    outs = start_all(scatter_copies(spot[1], part, 2, 0, PAD, *parts, part_sems, first=1))
    wait_all(gu)
    rows = row_outs(out, in_own, in_first, in_rest, out_sems)
    for n in (3, 2, 1, 0):
        at = pl.ds(n * STEP, STEP)
        out[at, :] = contract(pre_grad[at, :], w_gu[...], (1, 1)).astype(BF)
    start_all(rows)
    wait_all(outs)
    wait_all(rows)


def pass_kernel(keep_a, got_a, keep_b, got_b, up_a, up_b, out_a, out_b, ins, sums, in_sems, out_sems):
    loads = [
        pltpu.make_async_copy(ref.at[1], ins.at[n], in_sems.at[n]) for n, ref in enumerate((keep_a, got_a, keep_b, got_b))
    ]
    start_all(loads)
    wait_all(loads)
    for n in range(2):
        sums[n] = (ins[2 * n].astype(F32) + ins[2 * n + 1].astype(F32)).astype(BF)
    stores = [pltpu.make_async_copy(sums.at[n], ref.at[0], out_sems.at[n]) for n, ref in enumerate((out_b, out_a))]
    start_all(stores)
    wait_all(stores)


def finish_rows_kernel(spread, keep, got, out_t):
    width = out_t.shape[0]
    total = (keep[...].astype(F32) + got[...].astype(F32)).T
    if spread:
        block = width // 8
        total = jnp.concatenate([total[i * PAD : i * PAD + block] for i in range(8)], axis=0)
    out_t[...] = total[:width].astype(BF)


def finish_gate_up_kernel(spot, gate_keep, gate_far, up_keep, up_far, out):
    core = spot[0]
    block = out.shape[0]
    parts = []
    for keep, far in ((gate_keep, gate_far), (up_keep, up_far)):
        mine = keep[...].astype(F32)[:block]
        theirs = far[...].astype(F32)[:block]
        even = jnp.where(core == 0, mine, theirs)
        odd = jnp.where(core == 0, theirs, mine)
        for j in range(4):
            for p in (even, odd):
                at = j * PAD
                parts += [p[:, at : at + MAIN], p[:, at + 164 : at + 176], p[:, at + 180 : at + PAD]]
    out[...] = jnp.concatenate(parts, axis=1).reshape(out.shape)


def finish_down_kernel(keep_a, got_a, last_a, keep_b, got_b, last_b, out):
    def total(keep, got, last):
        return keep[0].astype(F32) + got[0].astype(F32) + last[...].astype(F32)

    rows = jnp.concatenate([total(keep_a, got_a, last_a), total(keep_b, got_b, last_b)], axis=0)
    rows = jnp.concatenate([rows[:MAIN], rows[164:176], rows[180:]], axis=0)
    out[...] = rows[:, : out.shape[2]].reshape(out.shape)


VMEM = pl.BlockSpec(memory_space=pltpu.VMEM)
SMEM = pl.BlockSpec(memory_space=pltpu.SMEM)
ANY = pl.BlockSpec(memory_space=pl.ANY)


def call(body, in_specs, out_specs, out_shape, scratch=(), mib=58, flops=1000, aliases=None):
    return pl.pallas_call(
        body,
        in_specs=in_specs,
        out_specs=out_specs,
        out_shape=out_shape,
        scratch_shapes=list(scratch),
        input_output_aliases=aliases or {},
        compiler_params=pltpu.CompilerParams(vmem_limit_bytes=mib * MIB),
        cost_estimate=pl.CostEstimate(flops=flops, bytes_accessed=1000, transcendentals=0),
    )


def paired(tokens, expert_ids, combine_weights, out_grad, w_gate_up, w_down):
    count, top = expert_ids.shape
    width = tokens.shape[1]
    scale = 1.0 / math.sqrt(8 * count * top)
    place = lax.axis_index("dp")
    line = lax.axis_index("expert")
    core = place % 2
    spot = jnp.stack([core, place // 2, line]).astype(jnp.int32)
    block = w_gate_up.shape[1]
    full = 8 * PAD
    units = 4 * PAD
    rows = 8 * count
    dma = pltpu.SemaphoreType.DMA

    def swap(bit):
        pairs = [(i, i ^ bit) for i in range(8)]
        return lambda value: lax.ppermute(value, "dp", pairs)

    over_core, over_x, over_y = swap(1), swap(2), swap(4)

    def onward(value):
        return lax.ppermute(value, "expert", [(i, (i + 1) % 4) for i in range(4)])

    def backward(value):
        return lax.ppermute(value, "expert", [(i, (i + 3) % 4) for i in range(4)])

    def array(*shape):
        return jax.ShapeDtypeStruct(shape, BF)

    def held(*shape):
        return pltpu.VMEM(shape, BF)

    def together(*values):
        return lax.optimization_barrier(values)

    xg0, own, other, high = call(
        prepare_kernel,
        [SMEM] + [VMEM] * 6,
        [VMEM] * 4,
        [array(count, 2 * full), array(PAD + LOT, full), array(PAD, full), array(LOT, full)],
    )(spot, tokens.T, out_grad.T, expert_ids.T, combine_weights.T, w_gate_up[0], w_down[0])

    other, own_x, own_y, xg1, fxg0 = over_core(other), over_x(own), over_y(own), onward(xg0), over_core(xg0)
    other = call(join_kernel, [VMEM] * 3, VMEM, array(PAD + LOT, full))(other, high, w_down[0])
    own_x, own_y, xg1, other, fxg0 = together(own_x, own_y, xg1, other, fxg0)
    other_x, other_y, xg2, fxg1 = over_x(other), over_y(other), onward(xg1), over_core(xg1)
    other_x, other_y, xg2, fxg1, own_x = together(other_x, other_y, xg2, fxg1, own_x)
    own_xy, other_xy, xg3, fxg2 = over_y(own_x), over_x(other_y), onward(xg2), over_core(xg2)
    fxg3 = over_core(xg3)

    owns = (own, own_x, own_y, own_xy)
    others = (other, other_x, other_y, other_xy)
    xs = (xg0, xg1, xg2, xg3, fxg0, fxg1, fxg2, fxg3)
    row_shapes = [array(rows // 2, full), array(count, full), array(3 * count, full)]
    up_f, gate_f, grad, out_own, out_first, out_rest, *down_parts = call(
        functools.partial(forward_kernel, scale),
        [SMEM] + [ANY] * 16,
        [ANY] * 10,
        [array(rows, units)] * 2 + [array(rows, full)] + row_shapes + [array(2, HALF, full)] * 4,
        [held(full, full), held(units, full), held(rows, full), held(rows, full)]
        + [held(rows, units)] * 3
        + [pltpu.VMEM((rows, 128), F32), held(rows, full), held(units, full)]
        + [dma((8,)), dma((16,)), dma((8,)), dma((8,)), dma((12,)), dma((3,)), dma((8,))],
        flops=LONG,
    )(spot, *owns, *others, *xs)

    def slot_sum(own_part, far_part, s, far):
        return own_part[s * count : (s + 1) * count].astype(F32) + far_part[far * count : (far + 1) * count].astype(F32)

    def after(value, moving):
        return (value + moving.astype(F32)).astype(BF)

    def first_step(parts):
        return over_x(parts[0]), over_y(parts[2])

    def passed_on(parts, got):
        def add(a, b):
            return (a[1].astype(F32) + b[1].astype(F32)).astype(BF)

        return add(parts[1], got[0]), add(parts[3], got[1])

    def second_step(away):
        return over_y(away[0]), over_x(away[1])

    def totals(parts, got, last):
        def add(a, b, c):
            return a[0].astype(F32) + b[0].astype(F32) + c.astype(F32)

        return add(parts[1], got[0], last[0]), add(parts[3], got[1], last[1])

    down_got = first_step(down_parts)
    m1 = slot_sum(out_own, over_core(out_first), 3, 0).astype(BF)
    m1, grad = together(m1, grad)
    m1 = backward(m1)
    out_rest = over_core(out_rest)
    pre_grad, *gate_parts = call(
        functools.partial(gate_grad_kernel, scale),
        [SMEM] + [ANY] * 19,
        [ANY] * 5,
        [array(rows, full)] + [array(2, PAD, units)] * 4,
        [held(units, full), held(rows, full), held(rows, units), held(rows, units), held(rows, full)]
        + [held(rows, full), held(full, units), dma((16,)), dma((12,)), dma((8,)), dma((4,)), dma((8,))],
        flops=LONG,
    )(spot, *owns, *others, grad, up_f, gate_f, *xs)
    *down_got, m1, pre_grad, gate_a, gate_b, out_rest = together(
        *down_got, m1, pre_grad, gate_parts[0], gate_parts[2], out_rest
    )
    m2 = backward(after(slot_sum(out_own, out_rest, 2, 2), m1))
    down_last = second_step(passed_on(down_parts, down_got))
    gate_got = over_x(gate_a), over_y(gate_b)
    in_own, in_first, in_rest, *up_parts = call(
        functools.partial(up_grad_kernel, scale),
        [SMEM] + [ANY] * 17,
        [ANY] * 7,
        row_shapes + [array(3, PAD, units), array(2, PAD, units)] * 2,
        [held(full, full), held(rows, full), held(rows, full), held(full, units), held(rows, full)]
        + [dma((8,)), dma((8,)), dma((4,)), dma((4,)), dma((8,))],
        flops=LONG,
    )(spot, *owns, *others, *xs, pre_grad)
    m2, in_first, in_rest, l1, l2, g1, g2, up_a, up_b = together(
        m2, in_first, in_rest, *down_last, *gate_got, up_parts[0], up_parts[2]
    )
    down_last, gate_got = (l1, l2), (g1, g2)
    m3 = after(slot_sum(out_own, out_rest, 1, 1), m2)
    up_a, up_b = call(
        pass_kernel,
        [ANY] * 6,
        [ANY] * 2,
        [array(3, PAD, units)] * 2,
        [held(4, PAD, units), held(2, PAD, units), dma((4,)), dma((2,))],
        aliases={4: 0, 5: 1},
    )(gate_parts[1], gate_got[0], gate_parts[3], gate_got[1], up_a, up_b)
    up_a, up_b, m3, in_first, in_rest = together(up_a, up_b, m3, in_first, in_rest)
    by_y, by_x, m3 = over_y(up_b), over_x(up_a), backward(m3)
    i1 = backward(slot_sum(in_own, over_core(in_first), 3, 0).astype(BF))
    in_rest = over_core(in_rest)

    def finish_rows(value, moving, spread):
        return call(functools.partial(finish_rows_kernel, spread), [VMEM] * 2, VMEM, array(width, count))(value, moving).T

    grad_down = call(
        finish_down_kernel, [VMEM] * 6, VMEM, jax.ShapeDtypeStruct((block, 1, width), F32)
    )(down_parts[1], down_got[0], down_last[0], down_parts[3], down_got[1], down_last[1])
    by_x, by_y, m3, grad_down = together(by_x, by_y, m3, grad_down)
    up_got, gate_last = (by_x[1:], by_y[1:]), (by_y[0], by_x[0])
    i2 = backward(after(slot_sum(in_own, in_rest, 2, 2), i1))
    up_last = second_step(passed_on(up_parts, up_got))

    def split(parts, got, last):
        a, b = totals(parts, got, last)
        return jnp.where(core == 0, a, b), over_core(jnp.where(core == 0, b, a).astype(BF))

    gate_keep, gate_far = split(gate_parts, gate_got, gate_last)
    i3 = after(slot_sum(in_own, in_rest, 1, 1), i2)
    mixed_out = finish_rows(slot_sum(out_own, out_rest, 0, 0), m3, False)
    l1, l2, gate_keep, gate_far, mixed_out, _ = together(*up_last, gate_keep, gate_far, mixed_out, i3)
    i3 = backward(i3)
    up_keep, up_far = split(up_parts, up_got, (l1, l2))
    grad_gate_up = call(
        finish_gate_up_kernel,
        [SMEM] + [VMEM] * 4,
        VMEM,
        jax.ShapeDtypeStruct((block, 1, 2 * width), F32),
    )(spot, gate_keep, gate_far, up_keep, up_far)
    token_grad = finish_rows(slot_sum(in_own, in_rest, 0, 0), i3, True)
    return (mixed_out, token_grad, grad_gate_up.transpose(1, 0, 2), grad_down.transpose(1, 0, 2))


def solution(mesh):
    placed = (
        P(("dp", "expert"), None),
        P(("dp", "expert"), None),
        P(("dp", "expert"), None),
        P(("dp", "expert"), None),
        P("expert", "dp", None),
        P("expert", "dp", None),
    )
    small = mesh.shape["dp"] == 8 and mesh.shape["expert"] == 4
    return jax.shard_map(
        paired if small else general,
        mesh=mesh,
        in_specs=placed,
        out_specs=(
            P(("dp", "expert"), None),
            P(("dp", "expert"), None),
            P("expert", "dp", None),
            P("expert", "dp", None),
        ),
        check_vma=False,
    )
```

time: 213 us -> 191 us (0.90)
  starting transfers between devices: 46.4 us -> 31.2 us
  local copies, waits for them, and re-layouts: 11.4 us -> 3 us
  waiting for transfers between devices: 73.3 us -> 81.2 us
  other arithmetic: 15.2 us -> 10.3 us
    ppermute x4 -> x3, waiting for transfers between devices: 20.1 us -> 52.4 us  [onward(): return lax.ppermute(value, 'expert', [(i, (i + 1) % 4) for i in range(4)])]
    ppermute x37 -> x27, waiting for transfers between devices: 33.3 us -> 19.1 us  [swap(): return lambda value: lax.ppermute(value, 'dp', pairs)]
    ppermute x6, waiting for transfers between devices: 19.9 us -> 9.68 us  [backward(): return lax.ppermute(value, 'expert', [(i, (i + 3) % 4) for i in range(4)])]
    unnamed x86 -> x70, local copies, waits for them, and re-layouts: 11.3 us -> 3 us
    ppermute x6, starting transfers between devices: 14.6 us -> 7.36 us  [backward(): return lax.ppermute(value, 'expert', [(i, (i + 3) % 4) for i in range(4)])]
    ppermute x37 -> x27, starting transfers between devices: 28.3 us -> 22.2 us  [swap(): return lambda value: lax.ppermute(value, 'dp', pairs)]
    convert_element_type x6 -> x2, other arithmetic: 3.98 us -> 0.14 us  [add(): return (a[1].astype(F32) + b[1].astype(F32)).astype(BF)]
    select_n x0 -> x1, other arithmetic: none -> 2.54 us  [split(): jnp.where(core == 0, b, a).astype(BF)]
  transfers between devices with their start and end apart: 47 -> 36, of which waited for: 21 -> 17; matrix products, arithmetic and copies ran while one was open for 10% -> 4% of each run, Pallas kernels for 28% -> 19%
where the time goes in v1:
time: 191 us; the launch traced here: 190 us
  waiting for transfers between devices  81.2 us (43%)
  Pallas kernels  63.4 us (33%)
  starting transfers between devices  31.2 us (16%)
  other arithmetic  10.3 us (5%)
  local copies, waits for them, and re-layouts  3 us (2%)
    ppermute x3, waiting for transfers between devices, onward(): return lax.ppermute(value, 'expert', [(i, (i + 1) % 4) for i in range(4)])  52.4 us
    ppermute x27, starting transfers between devices, swap(): return lambda value: lax.ppermute(value, 'dp', pairs)  22.2 us
    ppermute x27, waiting for transfers between devices, swap(): return lambda value: lax.ppermute(value, 'dp', pairs)  19.1 us
    pallas_call x1, Pallas kernels, paired(): call(functools.partial(forward_kernel, scale), [SMEM] + [ANY] * 16, [ANY]...  17.7 us
    pallas_call x1, Pallas kernels, paired(): call(functools.partial(up_grad_kernel, scale), [SMEM] + [ANY] * 17, [ANY]...  13.1 us
    pallas_call x1, Pallas kernels, paired(): call(functools.partial(gate_grad_kernel, scale), [SMEM] + [ANY] * 19, [AN...  11.7 us
    ppermute x6, waiting for transfers between devices, backward(): return lax.ppermute(value, 'expert', [(i, (i + 3) % 4) for i in range(4)])  9.68 us
    ppermute x6, starting transfers between devices, backward(): return lax.ppermute(value, 'expert', [(i, (i + 3) % 4) for i in range(4)])  7.36 us
  transfers between devices with their start and end apart: 36, of which 17 were waited for; matrix products, arithmetic and copies ran while one was open for 4% of the time, Pallas kernels for 19%

profile of v1, /device:TPU:0, one launch (start us, length us, event | category | flops | bytes accessed | tf_op | source)
XLA Modules:
  0.0 190.1 jit_solution(12725564813323329936)
XLA Ops:
  1.2 4.1 %shard_map.93 = (bf16[128,3072]{1,0:T(8,128)(2,1)}, bf16[272,1536]{1,0:T(8,128)(2,1)}, bf16[192,1536]{1,0:T(8,128)(2,1)}, bf16[80,1536]{1,0:T(8,128)(2,1)}) custom-call(s32[3]{0:T(128)} %pad_add_fusion.spot.refs_0_, bf16[1440,128]{1,0:T(8,128)(2,1)} %bitcast.42, bf16[1440,128]{1,0:T(8,128)(2,1)} %bitcast.43, s32[2,128]{1,0:T(2,128)} %bitcast.46, ...), custom_call_target="tpu_custom_call" | custom-call | flops 1000 | bytes 1000 | tf_op jit(solution)/shard_map/pallas_call | solution.py:430
  5.3 3.0 %collective-permute-start.1 = (bf16[272,1536]{1,0:T(8,128)(2,1)}, bf16[272,1536]{1,0:T(8,128)(2,1)S(1)}, u32[]{:S(2)}, u32[]{:S(2)}) collective-permute-start(bf16[272,1536]{1,0:T(8,128)(2,1)} %get-tuple-element.74.refs_1_), channel_id=1, source_target_pairs={{0,16},{4,20},{8,24},{12,28},{16,0},{20,4},{24,8},{28,12},{1,17},{... | collective-permute-start | bytes 2506760 | tf_op jit(solution)/shard_map/ppermute | solution.py:411
  11.6 2.0 %collective-permute-done.3.other = bf16[192,1536]{1,0:T(8,128)(2,1)S(1)} collective-permute-done((bf16[192,1536]{1,0:T(8,128)(2,1)}, bf16[192,1536]{1,0:T(8,128)(2,1)S(1)}, u32[]{:S(2)}, u32[]{:S(2)}) %collective-permute-start.3) | collective-permute-done | bytes 589856 | tf_op jit(solution)/shard_map/ppermute | solution.py:411
  14.4 2.3 %shard_map.94.refs_5_ = bf16[272,1536]{1,0:T(8,128)(2,1)} custom-call(bf16[192,1536]{1,0:T(8,128)(2,1)} %copy-done.16, bf16[80,1536]{1,0:T(8,128)(2,1)} %get-tuple-element.77.high, bf16[180,1440]{1,0:T(8,128)(2,1)} %bitcast.38), custom_call_target="tpu_custom_call" | custom-call | flops 1000 | bytes 1000 | tf_op jit(solution)/shard_map/pallas_call | solution.py:438
  16.7 15.1 %collective-permute-done.2.refs_10_.refs_13_ = bf16[128,3072]{1,0:T(8,128)(2,1)S(1)} collective-permute-done((bf16[128,3072]{1,0:T(8,128)(2,1)}, bf16[128,3072]{1,0:T(8,128)(2,1)S(1)}, u32[]{:S(2)}, u32[]{:S(2)}) %collective-permute-start.2) | collective-permute-done | bytes 786464 | tf_op jit(solution)/shard_map/ppermute | solution.py:416
  33.0 2.3 %collective-permute-done.8.refs_14_.refs_17_ = bf16[128,3072]{1,0:T(8,128)(2,1)S(1)} collective-permute-done((bf16[128,3072]{1,0:T(8,128)(2,1)S(1)}, bf16[128,3072]{1,0:T(8,128)(2,1)S(1)}, u32[]{:S(2)}, u32[]{:S(2)}) %collective-permute-start.8) | collective-permute-done | bytes 786464 | tf_op jit(solution)/shard_map/ppermute | solution.py:411
  35.2 19.5 %collective-permute-done.7.refs_11_.refs_14_ = bf16[128,3072]{1,0:T(8,128)(2,1)S(1)} collective-permute-done((bf16[128,3072]{1,0:T(8,128)(2,1)S(1)}, bf16[128,3072]{1,0:T(8,128)(2,1)S(1)}, u32[]{:S(2)}, u32[]{:S(2)}) %collective-permute-start.7) | collective-permute-done | bytes 786464 | tf_op jit(solution)/shard_map/ppermute | solution.py:416
  57.9 17.9 %collective-permute-done.11.refs_12_.refs_15_ = bf16[128,3072]{1,0:T(8,128)(2,1)S(1)} collective-permute-done((bf16[128,3072]{1,0:T(8,128)(2,1)S(1)}, bf16[128,3072]{1,0:T(8,128)(2,1)S(1)}, u32[]{:S(2)}, u32[]{:S(2)}) %collective-permute-start.11) | collective-permute-done | bytes 786464 | tf_op jit(solution)/shard_map/ppermute | solution.py:416
  78.2 17.7 %shard_map.95 = (bf16[1024,768]{1,0:T(8,128)(2,1)}, bf16[1024,768]{1,0:T(8,128)(2,1)}, bf16[1024,1536]{1,0:T(8,128)(2,1)}, bf16[512,1536]{1,0:T(8,128)(2,1)}, bf...) custom-call(s32[3]{0:T(128)} %pad_add_fusion.spot.refs_0_, ...), custom_call_target="tpu_custom_call" | custom-call | flops 30000001024 | bytes 1000 | tf_op jit(solution)/shard_map/pallas_call | solution.py:449
  100.3 1.6 collective-permute-start.17
  101.9 11.7 %shard_map.96 = (bf16[1024,1536]{1,0:T(8,128)(2,1)}, bf16[2,192,768]{2,1,0:T(8,128)(2,1)}, bf16[2,192,768]{2,1,0:T(8,128)(2,1)}, bf16[2,192,768]{2,1,0:T(8,128)(2,1)}, bf16[2,192,768]{2,1,0:T(8,128)(2,1)}) custom-call(s32[3]{0:T(128)} %pad_add_fusion.spot.refs_0_, bf16[272,1536]{1,0:T(8,128)(2,1)} %get-tuple-element.74.refs_1_, ...), custom_call_target="tpu_custom_call" | custom-call | flops 30000001024 | bytes 1000 | tf_op jit(solution)/shard_map/pallas_call | solution.py:490
  120.3 13.1 %shard_map.97 = (bf16[512,1536]{1,0:T(8,128)(2,1)}, bf16[128,1536]{1,0:T(8,128)(2,1)}, bf16[384,1536]{1,0:T(8,128)(2,1)}, bf16[3,192,768]{2,1,0:T(8,128)(2,1)}, ...) custom-call(s32[3]{0:T(128)} %pad_add_fusion.spot.refs_0_, ...), custom_call_target="tpu_custom_call" | custom-call | flops 30000001024 | bytes 1000 | tf_op jit(solution)/shard_map/pallas_call | solution.py:505
  133.4 2.2 %collective-permute-done.22.got_a = bf16[2,192,768]{2,1,0:T(8,128)(2,1)S(1)} collective-permute-done((bf16[2,192,768]{2,1,0:T(8,128)(2,1)}, bf16[2,192,768]{2,1,0:T(8,128)(2,1)S(1)}, u32[]{:S(2)}, u32[]{:S(2)}) %collective-permute-start.22) | collective-permute-done | bytes 589856 | tf_op jit(solution)/shard_map/ppermute | solution.py:411
  137.7 2.4 %shard_map.98 = (bf16[3,192,768]{2,1,0:T(8,128)(2,1)}, bf16[3,192,768]{2,1,0:T(8,128)(2,1)}) custom-call(bf16[2,192,768]{2,1,0:T(8,128)(2,1)} %get-tuple-element.103.keep_a, bf16[2,192,768]{2,1,0:T(8,128)(2,1)} %copy-done.4, bf16[2,192,768]{2,1,0:T(8,128)(2,1)} %get-tuple-element.117.keep_b, ...), custom_call_target="tpu_custom_call", output_to_operand_aliasing={{0}: (4, {}), {1}: (5, {})} | custom-call | flops 1000 | bytes 1000 | tf_op jit(solution)/shard_map/pallas_call | solution.py:519
  146.0 8.2 %collective-permute-done.32 = bf16[128,1536]{1,0:T(8,128)(2,1)S(1)} collective-permute-done((bf16[128,1536]{1,0:T(8,128)(2,1)S(1)}, bf16[128,1536]{1,0:T(8,128)(2,1)S(1)}, u32[]{:S(2)}, u32[]{:S(2)}) %collective-permute-start.32) | collective-permute-done | bytes 393248 | tf_op jit(solution)/shard_map/ppermute | solution.py:419
  155.5 2.6 %collective-permute-start.33 = (bf16[128,1536]{1,0:T(8,128)(2,1)}, bf16[128,1536]{1,0:T(8,128)(2,1)}, u32[]{:S(2)}, u32[]{:S(2)}) collective-permute-start(bf16[128,1536]{1,0:T(8,128)(2,1)} %get-tuple-element.149), channel_id=1, source_target_pairs={{0,3},{1,0},{2,1},{3,2},{4,7},{5,4},{6,5},{7,6},{8,11},{9,8},{10,9... | collective-permute-start | bytes 1179656 | tf_op jit(solution)/shard_map/ppermute | solution.py:419
  158.0 3.3 %shard_map.99 = f32[180,1,1440]{2,1,0:T(1,128)} custom-call(bf16[2,96,1536]{2,1,0:T(8,128)(2,1)} %get-tuple-element.108.keep_a, bf16[2,96,1536]{2,1,0:T(8,128)(2,1)} %copy-done.10, bf16[96,1536]{1,0:T(8,128)(2,1)} %collective-permute-done.20.last_a, bf16[2,96,1536]{2,1,0:T(8,128)(2,1)} %get-tuple-element.110.keep_b, bf16[2,96,1536]{2,1,0:T(8,128)(2,1)} %copy-done.11, ...), custom_call_target="tpu_custom_call" | custom-call | flops 1000 | bytes 1000 | tf_op jit(solution)/shard_map/pallas_call | solution.py:535
  162.8 2.0 %collective-permute-done.24 = bf16[3,192,768]{2,1,0:T(8,128)(2,1)} collective-permute-done((bf16[3,192,768]{2,1,0:T(8,128)(2,1)}, bf16[3,192,768]{2,1,0:T(8,128)(2,1)}, u32[]{:S(2)}, u32[]{:S(2)}) %collective-permute-start.24) | collective-permute-done | bytes 884768 | tf_op jit(solution)/shard_map/ppermute | solution.py:411
  165.9 2.5 %fusion.5 = (bf16[192,768]{1,0:T(8,128)(2,1)}, f32[192,768]{1,0:T(8,128)}, bf16[192,768]{1,0:T(8,128)(2,1)}, bf16[192,768]{1,0:T(8,128)(2,1)S(1)}) fusion(pred[]{:T(512)S(6)} %eq.4, bf16[3,192,768]{2,1,0:T(8,128)(2,1)} %collective-permute-done.24, bf16[2,192,768]{2,1,0:T(8,128)(2,1)S(1)} %copy-done.7, bf16[2,192,768]{2,1,0:T(8,128)(2,1)S(1)} %copy-done.3, ...), kind=kLoop, calls=%fused_computation.24 | loop fusion | flops 3096576 | bytes 4423681 | tf_op jit(solution)/shard_map/jit(_where)/select_n | solution.py:545
  170.5 2.2 %shard_map.100 = bf16[1440,128]{1,0:T(8,128)(2,1)} custom-call(f32[128,1536]{1,0:T(8,128)} %get-tuple-element.150.keep, bf16[128,1536]{1,0:T(8,128)(2,1)} %collective-permute-done.26.got), custom_call_target="tpu_custom_call" | custom-call | flops 1000 | bytes 1000 | tf_op jit(solution)/shard_map/pallas_call | solution.py:533
  174.2 3.9 %collective-permute-done.28 = bf16[192,768]{1,0:T(8,128)(2,1)S(1)} collective-permute-done((bf16[192,768]{1,0:T(8,128)(2,1)}, bf16[192,768]{1,0:T(8,128)(2,1)S(1)}, u32[]{:S(2)}, u32[]{:S(2)}) %collective-permute-start.28) | collective-permute-done | bytes 294944 | tf_op jit(solution)/shard_map/ppermute | solution.py:411
  178.2 2.1 %select_convert_fusion = (bf16[192,768]{1,0:T(8,128)(2,1)S(1)}, f32[192,768]{1,0:T(8,128)}) fusion(bf16[192,768]{1,0:T(8,128)(2,1)S(1)} %collective-permute-done.27, bf16[192,768]{1,0:T(8,128)(2,1)S(1)} %collective-permute-done.28, pred[]{:T(512)S(6)} %eq.4, bf16[3,192,768]{2,1,0:T(8,128)(2,1)} %collective-permute-done.25, ...), kind=kLoop, calls=%fused_computation.10 | loop fusion | flops 1916928 | bytes 2654209 | tf_op jit(solution)/shard_map/convert_element_type | solution.py:545
  182.7 4.5 %shard_map.102 = f32[180,1,2880]{2,1,0:T(1,128)} custom-call(s32[3]{0:T(128)} %pad_add_fusion.spot.refs_0_, f32[192,768]{1,0:T(8,128)} %get-tuple-element.139.gate_keep, bf16[192,768]{1,0:T(8,128)(2,1)} %copy-done.18, f32[192,768]{1,0:T(8,128)} %get-tuple-element.147.up_keep, bf16[192,768]{1,0:T(8,128)(2,1)} %copy-done.19), custom_call_target="tpu_custom_call" | custom-call | flops 1000 | bytes 1000 | tf_op jit(solution)/shard_map/pallas_call | solution.py:553
  187.9 2.1 %shard_map.101 = bf16[1440,128]{1,0:T(8,128)(2,1)} custom-call(f32[128,1536]{1,0:T(8,128)} %get-tuple-element.148.keep, bf16[128,1536]{1,0:T(8,128)(2,1)} %copy-done.17), custom_call_target="tpu_custom_call" | custom-call | flops 1000 | bytes 1000 | tf_op jit(solution)/shard_map/pallas_call | solution.py:533
  (139 shorter events, 40.8 us)
Async XLA Ops:
  5.3 26.5 %collective-permute-start.1 = (bf16[272,1536]{1,0:T(8,128)(2,1)}, bf16[272,1536]{1,0:T(8,128)(2,1)S(1)}, u32[]{:S(2)}, u32[]{:S(2)}) collective-permute-start(bf16[272,1536]{1,0:T(8,128)(2,1)} %get-tuple-element.74.refs_1_), channel_id=1, source_target_pairs={{0,16},{4,20},{8,24},{12,28},{16,0},{20,4},{24,8},{28,12},{1,17},{... | collective-permute-start | bytes 2506760 | tf_op jit(solution)/shard_map/ppermute | solution.py:411
  8.3 23.5 %collective-permute-start = (bf16[272,1536]{1,0:T(8,128)(2,1)}, bf16[272,1536]{1,0:T(8,128)(2,1)S(1)}, u32[]{:S(2)}, u32[]{:S(2)}) collective-permute-start(bf16[272,1536]{1,0:T(8,128)(2,1)} %get-tuple-element.74.refs_1_), channel_id=1, source_target_pairs={{0,8},{4,12},{8,0},{12,4},{16,24},{20,28},{24,16},{28,20},{1,9},{5... | collective-permute-start | bytes 2506760 | tf_op jit(solution)/shard_map/ppermute | solution.py:411
  9.8 22.0 %collective-permute-start.2 = (bf16[128,3072]{1,0:T(8,128)(2,1)}, bf16[128,3072]{1,0:T(8,128)(2,1)S(1)}, u32[]{:S(2)}, u32[]{:S(2)}) collective-permute-start(bf16[128,3072]{1,0:T(8,128)(2,1)} %get-tuple-element.75.refs_9_.refs_12_), channel_id=1, source_target_pairs={{0,1},{1,2},{2,3},{3,0},{4,5},{5,6},{6,7},{7,4},{8,9},{9,10},{10,1... | collective-permute-start | bytes 2359304 | tf_op jit(solution)/shard_map/ppermute | solution.py:416
  31.8 22.9 %collective-permute-start.6 = (bf16[272,1536]{1,0:T(8,128)(2,1)}, bf16[272,1536]{1,0:T(8,128)(2,1)S(1)}, u32[]{:S(2)}, u32[]{:S(2)}) collective-permute-start(bf16[272,1536]{1,0:T(8,128)(2,1)} %shard_map.94.refs_5_), channel_id=1, source_target_pairs={{0,16},{4,20},{8,24},{12,28},{16,0},{20,4},{24,8},{28,12},{1,17},{... | collective-permute-start | bytes 2506760 | tf_op jit(solution)/shard_map/ppermute | solution.py:411
  32.4 22.3 %collective-permute-start.5 = (bf16[272,1536]{1,0:T(8,128)(2,1)}, bf16[272,1536]{1,0:T(8,128)(2,1)S(1)}, u32[]{:S(2)}, u32[]{:S(2)}) collective-permute-start(bf16[272,1536]{1,0:T(8,128)(2,1)} %shard_map.94.refs_5_), channel_id=1, source_target_pairs={{0,8},{4,12},{8,0},{12,4},{16,24},{20,28},{24,16},{28,20},{1,9},{5... | collective-permute-start | bytes 2506760 | tf_op jit(solution)/shard_map/ppermute | solution.py:411
  32.9 21.8 %collective-permute-start.7 = (bf16[128,3072]{1,0:T(8,128)(2,1)S(1)}, bf16[128,3072]{1,0:T(8,128)(2,1)S(1)}, u32[]{:S(2)}, u32[]{:S(2)}) collective-permute-start(bf16[128,3072]{1,0:T(8,128)(2,1)S(1)} %collective-permute-done.2.refs_10_.refs_13_), channel_id=1, source_target_pairs={{0,1},{1,2},{2,3},{3,0},{4,5},{5,6},{6,7},{7,4},{8,9},{9,10},{10,1... | collective-permute-start | bytes 2359304 | tf_op jit(solution)/shard_map/ppermute | solution.py:416
  54.7 21.0 %collective-permute-start.11 = (bf16[128,3072]{1,0:T(8,128)(2,1)S(1)}, bf16[128,3072]{1,0:T(8,128)(2,1)S(1)}, u32[]{:S(2)}, u32[]{:S(2)}) collective-permute-start(bf16[128,3072]{1,0:T(8,128)(2,1)S(1)} %collective-permute-done.7.refs_11_.refs_14_), channel_id=1, source_target_pairs={{0,1},{1,2},{2,3},{3,0},{4,5},{5,6},{6,7},{7,4},{8,9},{9,10},{10,1... | collective-permute-start | bytes 2359304 | tf_op jit(solution)/shard_map/ppermute | solution.py:416
  54.8 21.0 %collective-permute-start.9 = (bf16[272,1536]{1,0:T(8,128)(2,1)S(1)}, bf16[272,1536]{1,0:T(8,128)(2,1)S(1)}, u32[]{:S(2)}, u32[]{:S(2)}) collective-permute-start(bf16[272,1536]{1,0:T(8,128)(2,1)S(1)} %collective-permute-done.refs_2_), channel_id=1, source_target_pairs={{0,16},{4,20},{8,24},{12,28},{16,0},{20,4},{24,8},{28,12},{1,17},{... | collective-permute-start | bytes 2506760 | tf_op jit(solution)/shard_map/ppermute | solution.py:411
  56.4 19.9 %collective-permute-start.10 = (bf16[272,1536]{1,0:T(8,128)(2,1)S(1)}, bf16[272,1536]{1,0:T(8,128)(2,1)S(1)}, u32[]{:S(2)}, u32[]{:S(2)}) collective-permute-start(bf16[272,1536]{1,0:T(8,128)(2,1)S(1)} %collective-permute-done.6.refs_7_), channel_id=1, source_target_pairs={{0,8},{4,12},{8,0},{12,4},{16,24},{20,28},{24,16},{28,20},{1,9},{5... | collective-permute-start | bytes 2506760 | tf_op jit(solution)/shard_map/ppermute | solution.py:411
  57.9 17.9 %collective-permute-start.12 = (bf16[128,3072]{1,0:T(8,128)(2,1)S(1)}, bf16[128,3072]{1,0:T(8,128)(2,1)S(1)}, u32[]{:S(2)}, u32[]{:S(2)}) collective-permute-start(bf16[128,3072]{1,0:T(8,128)(2,1)S(1)} %collective-permute-done.7.refs_11_.refs_14_), channel_id=1, source_target_pairs={{0,4},{4,0},{8,12},{12,8},{16,20},{20,16},{24,28},{28,24},{1,5},{5... | collective-permute-start | bytes 2359304 | tf_op jit(solution)/shard_map/ppermute | solution.py:411
  96.1 17.5 %collective-permute-start.14 = (bf16[2,96,1536]{2,1,0:T(8,128)(2,1)}, bf16[2,96,1536]{2,1,0:T(8,128)(2,1)S(1)}, u32[]{:S(2)}, u32[]{:S(2)}) collective-permute-start(bf16[2,96,1536]{2,1,0:T(8,128)(2,1)} %get-tuple-element.88), channel_id=1, source_target_pairs={{0,8},{4,12},{8,0},{12,4},{16,24},{20,28},{24,16},{28,20},{1,9},{5... | collective-permute-start | bytes 1769480 | tf_op jit(solution)/shard_map/ppermute | solution.py:411
  97.6 16.0 %collective-permute-start.15 = (bf16[2,96,1536]{2,1,0:T(8,128)(2,1)}, bf16[2,96,1536]{2,1,0:T(8,128)(2,1)S(1)}, u32[]{:S(2)}, u32[]{:S(2)}) collective-permute-start(bf16[2,96,1536]{2,1,0:T(8,128)(2,1)} %get-tuple-element.89), channel_id=1, source_target_pairs={{0,16},{4,20},{8,24},{12,28},{16,0},{20,4},{24,8},{28,12},{1,17},{... | collective-permute-start | bytes 1769480 | tf_op jit(solution)/shard_map/ppermute | solution.py:411
  99.2 14.5 %collective-permute-start.18 = (bf16[384,1536]{1,0:T(8,128)(2,1)}, bf16[384,1536]{1,0:T(8,128)(2,1)S(1)}, u32[]{:S(2)}, u32[]{:S(2)}) collective-permute-start(bf16[384,1536]{1,0:T(8,128)(2,1)} %get-tuple-element.100), channel_id=1, source_target_pairs={{0,4},{4,0},{8,12},{12,8},{16,20},{20,16},{24,28},{28,24},{1,5},{5... | collective-permute-start | bytes 3538952 | tf_op jit(solution)/shard_map/ppermute | solution.py:411
  113.8 19.6 %collective-permute-start.21 = (bf16[96,1536]{1,0:T(8,128)(2,1)S(1)}, bf16[96,1536]{1,0:T(8,128)(2,1)S(1)}, u32[]{:S(2)}, u32[]{:S(2)}) collective-permute-start(bf16[96,1536]{1,0:T(8,128)(2,1)S(1)} %fusion.2), channel_id=1, source_target_pairs={{0,8},{4,12},{8,0},{12,4},{16,24},{20,28},{24,16},{28,20},{1,9},{5... | collective-permute-start | bytes 884744 | tf_op jit(solution)/shard_map/ppermute | solution.py:411
  115.2 18.2 %collective-permute-start.20 = (bf16[96,1536]{1,0:T(8,128)(2,1)S(1)}, bf16[96,1536]{1,0:T(8,128)(2,1)}, u32[]{:S(2)}, u32[]{:S(2)}) collective-permute-start(bf16[96,1536]{1,0:T(8,128)(2,1)S(1)} %fusion.1), channel_id=1, source_target_pairs={{0,16},{4,20},{8,24},{12,28},{16,0},{20,4},{24,8},{28,12},{1,17},{... | collective-permute-start | bytes 884744 | tf_op jit(solution)/shard_map/ppermute | solution.py:411
  116.2 17.2 %collective-permute-start.19 = (bf16[128,1536]{1,0:T(8,128)(2,1)S(1)}, bf16[128,1536]{1,0:T(8,128)(2,1)S(1)}, u32[]{:S(2)}, u32[]{:S(2)}) collective-permute-start(bf16[128,1536]{1,0:T(8,128)(2,1)S(1)} %add_convert_fusion.4), channel_id=1, source_target_pairs={{0,3},{1,0},{2,1},{3,2},{4,7},{5,4},{6,5},{7,6},{8,11},{9,8},{10,9... | collective-permute-start | bytes 1179656 | tf_op jit(solution)/shard_map/ppermute | solution.py:419
  117.8 17.8 %collective-permute-start.22 = (bf16[2,192,768]{2,1,0:T(8,128)(2,1)}, bf16[2,192,768]{2,1,0:T(8,128)(2,1)S(1)}, u32[]{:S(2)}, u32[]{:S(2)}) collective-permute-start(bf16[2,192,768]{2,1,0:T(8,128)(2,1)} %get-tuple-element.112), channel_id=1, source_target_pairs={{0,8},{4,12},{8,0},{12,4},{16,24},{20,28},{24,16},{28,20},{1,9},{5... | collective-permute-start | bytes 1769480 | tf_op jit(solution)/shard_map/ppermute | solution.py:411
  119.3 17.1 %collective-permute-start.23 = (bf16[2,192,768]{2,1,0:T(8,128)(2,1)}, bf16[2,192,768]{2,1,0:T(8,128)(2,1)S(1)}, u32[]{:S(2)}, u32[]{:S(2)}) collective-permute-start(bf16[2,192,768]{2,1,0:T(8,128)(2,1)} %get-tuple-element.113), channel_id=1, source_target_pairs={{0,16},{4,20},{8,24},{12,28},{16,0},{20,4},{24,8},{28,12},{1,17},{... | collective-permute-start | bytes 1769480 | tf_op jit(solution)/shard_map/ppermute | solution.py:411
  140.2 14.0 %collective-permute-start.30 = (bf16[384,1536]{1,0:T(8,128)(2,1)S(1)}, bf16[384,1536]{1,0:T(8,128)(2,1)S(1)}, u32[]{:S(2)}, u32[]{:S(2)}) collective-permute-start(bf16[384,1536]{1,0:T(8,128)(2,1)S(1)} %copy-done.21), channel_id=1, source_target_pairs={{0,4},{4,0},{8,12},{12,8},{16,20},{20,16},{24,28},{28,24},{1,5},{5... | collective-permute-start | bytes 3538952 | tf_op jit(solution)/shard_map/ppermute | solution.py:411
  143.0 21.7 %collective-permute-start.24 = (bf16[3,192,768]{2,1,0:T(8,128)(2,1)}, bf16[3,192,768]{2,1,0:T(8,128)(2,1)}, u32[]{:S(2)}, u32[]{:S(2)}) collective-permute-start(bf16[3,192,768]{2,1,0:T(8,128)(2,1)} %get-tuple-element.126), channel_id=1, source_target_pairs={{0,8},{4,12},{8,0},{12,4},{16,24},{20,28},{24,16},{28,20},{1,9},{5... | collective-permute-start | bytes 2654216 | tf_op jit(solution)/shard_map/ppermute | solution.py:411
  144.5 21.4 %collective-permute-start.25 = (bf16[3,192,768]{2,1,0:T(8,128)(2,1)}, bf16[3,192,768]{2,1,0:T(8,128)(2,1)}, u32[]{:S(2)}, u32[]{:S(2)}) collective-permute-start(bf16[3,192,768]{2,1,0:T(8,128)(2,1)} %get-tuple-element.127), channel_id=1, source_target_pairs={{0,16},{4,20},{8,24},{12,28},{16,0},{20,4},{24,8},{28,12},{1,17},{... | collective-permute-start | bytes 2654216 | tf_op jit(solution)/shard_map/ppermute | solution.py:411
  145.9 16.9 %collective-permute-start.26 = (bf16[128,1536]{1,0:T(8,128)(2,1)}, bf16[128,1536]{1,0:T(8,128)(2,1)}, u32[]{:S(2)}, u32[]{:S(2)}) collective-permute-start(bf16[128,1536]{1,0:T(8,128)(2,1)} %get-tuple-element.128), channel_id=1, source_target_pairs={{0,3},{1,0},{2,1},{3,2},{4,7},{5,4},{6,5},{7,6},{8,11},{9,8},{10,9... | collective-permute-start | bytes 1179656 | tf_op jit(solution)/shard_map/ppermute | solution.py:419
  155.5 17.2 %collective-permute-start.33 = (bf16[128,1536]{1,0:T(8,128)(2,1)}, bf16[128,1536]{1,0:T(8,128)(2,1)}, u32[]{:S(2)}, u32[]{:S(2)}) collective-permute-start(bf16[128,1536]{1,0:T(8,128)(2,1)} %get-tuple-element.149), channel_id=1, source_target_pairs={{0,3},{1,0},{2,1},{3,2},{4,7},{5,4},{6,5},{7,6},{8,11},{9,8},{10,9... | collective-permute-start | bytes 1179656 | tf_op jit(solution)/shard_map/ppermute | solution.py:419
  173.8 13.4 %collective-permute-start.34 = (bf16[128,1536]{1,0:T(8,128)(2,1)S(1)}, bf16[128,1536]{1,0:T(8,128)(2,1)S(1)}, u32[]{:S(2)}, u32[]{:S(2)}) collective-permute-start(bf16[128,1536]{1,0:T(8,128)(2,1)S(1)} %add_convert_fusion), channel_id=1, source_target_pairs={{0,3},{1,0},{2,1},{3,2},{4,7},{5,4},{6,5},{7,6},{8,11},{9,8},{10,9... | collective-permute-start | bytes 1179656 | tf_op jit(solution)/shard_map/ppermute | solution.py:419
  (47 other events, 446.3 us)

commit v2 on v1

--- a/solution.py
+++ b/solution.py
@@ -79,28 +79,32 @@
     return jnp.zeros(shape, dtype)
 
 
-def prepare_kernel(spot, tokens_t, grads_t, ids_t, weights_t, w_gu, w_down, packed, own, other, high):
+def prepare_rows_kernel(tokens_t, grads_t, ids_t, weights_t, packed):
+    width, count = tokens_t.shape
+    blocks = 8
+    block = width // blocks
+    full = blocks * PAD
+    x = tokens_t[...].astype(F32)
+    spread = []
+    for i in range(blocks):
+        spread += [x[i * block : (i + 1) * block], zeros((PAD - block, count))]
+    packed[:, :full] = jnp.concatenate(spread, axis=0).T.astype(BF)
+
+    hit = [ids_t[...] == e for e in range(4)]
+    table = jnp.concatenate(
+        [jnp.sum(jnp.where(h, weights_t[...], 0.0), axis=0, keepdims=True) for h in hit], axis=0
+    )
+    coarse = table.astype(BF).astype(F32)
+    rows = [grads_t[...].astype(F32), coarse, table - coarse, zeros((full - width - 8, count))]
+    packed[:, full:] = jnp.concatenate(rows, axis=0).T.astype(BF)
+
+
+def prepare_weights_kernel(spot, w_gu, w_down, own, other, high):
     core = spot[0]
-    width, count = tokens_t.shape
-    block = w_gu.shape[0]
+    block, width = w_down.shape
     blocks = width // block
     gap = PAD - block
     full = blocks * PAD
-
-    x = tokens_t[...].astype(F32)
-    spread = []
-    for i in range(blocks):
-        spread += [x[i * block : (i + 1) * block], zeros((gap, count))]
-    packed[:, :full] = jnp.concatenate(spread, axis=0).T.astype(BF)
-
-    hit = [ids_t[...] == e for e in range(4)]
-    table = jnp.concatenate(
-        [jnp.sum(jnp.where(h, weights_t[...], 0.0), axis=0, keepdims=True) for h in hit], axis=0
-    )
-    coarse = table.astype(BF).astype(F32)
-    rows = [grads_t[...].astype(F32), coarse, table - coarse, zeros((full - width - 8, count))]
-    packed[:, full:] = jnp.concatenate(rows, axis=0).T.astype(BF)
-
     w = w_gu[...]
     lot = block - MAIN
     edge = zeros((block, lot // 3), BF)
@@ -379,7 +383,7 @@
 ANY = pl.BlockSpec(memory_space=pl.ANY)
 
 
-def call(body, in_specs, out_specs, out_shape, scratch=(), mib=58, flops=1000, aliases=None):
+def call(body, in_specs, out_specs, out_shape, scratch=(), mib=50, flops=1000, aliases=None):
     return pl.pallas_call(
         body,
         in_specs=in_specs,
@@ -427,18 +431,22 @@
     def together(*values):
         return lax.optimization_barrier(values)
 
-    xg0, own, other, high = call(
-        prepare_kernel,
-        [SMEM] + [VMEM] * 6,
-        [VMEM] * 4,
-        [array(count, 2 * full), array(PAD + LOT, full), array(PAD, full), array(LOT, full)],
-    )(spot, tokens.T, out_grad.T, expert_ids.T, combine_weights.T, w_gate_up[0], w_down[0])
+    xg0 = call(prepare_rows_kernel, [VMEM] * 4, VMEM, array(count, 2 * full), mib=60)(
+        tokens.T, out_grad.T, expert_ids.T, combine_weights.T
+    )
+    own, other, high = call(
+        prepare_weights_kernel,
+        [SMEM] + [VMEM] * 2,
+        [VMEM] * 3,
+        [array(PAD + LOT, full), array(PAD, full), array(LOT, full)],
+        mib=60,
+    )(spot, w_gate_up[0], w_down[0])
 
     other, own_x, own_y, xg1, fxg0 = over_core(other), over_x(own), over_y(own), onward(xg0), over_core(xg0)
     other = call(join_kernel, [VMEM] * 3, VMEM, array(PAD + LOT, full))(other, high, w_down[0])
-    own_x, own_y, xg1, other, fxg0 = together(own_x, own_y, xg1, other, fxg0)
+    own_x, own_y, other, fxg0 = together(own_x, own_y, other, fxg0)
     other_x, other_y, xg2, fxg1 = over_x(other), over_y(other), onward(xg1), over_core(xg1)
-    other_x, other_y, xg2, fxg1, own_x = together(other_x, other_y, xg2, fxg1, own_x)
+    other_x, other_y, own_x = together(other_x, other_y, own_x)
     own_xy, other_xy, xg3, fxg2 = over_y(own_x), over_x(other_y), onward(xg2), over_core(xg2)
     fxg3 = over_core(xg3)
 

time: 191 us -> 181 us (0.948)
  waiting for transfers between devices: 81.2 us -> 69.5 us
  Pallas kernels: 63.4 us -> 56.9 us
  local copies, waits for them, and re-layouts: 3 us -> 9.19 us
  starting transfers between devices: 31.2 us -> 35.3 us
    ppermute x3, waiting for transfers between devices: 52.4 us -> 37.4 us  [onward(): return lax.ppermute(value, 'expert', [(i, (i + 1) % 4) for i in range(4)])]
    unnamed x70 -> x82, local copies, waits for them, and re-layouts: 3 us -> 9.19 us
    ppermute x6, starting transfers between devices: 7.36 us -> 11.6 us  [backward(): return lax.ppermute(value, 'expert', [(i, (i + 3) % 4) for i in range(4)])]
    ppermute x27, waiting for transfers between devices: 19.1 us -> 23.3 us  [swap(): return lambda value: lax.ppermute(value, 'dp', pairs)]
    pallas_call x1, Pallas kernels: 2.34 us -> 0.06 us  [paired(): call(join_kernel, [VMEM] * 3, VMEM, array(PAD + LOT, full))]
    pallas_call x1, Pallas kernels: 3.28 us -> 1.37 us  [paired(): call(finish_down_kernel, [VMEM] * 6, VMEM, jax.ShapeDtypeStruct((block, 1...]
    pallas_call x1 -> x2, Pallas kernels: 4.08 us -> 5.74 us  [the longest x1 3.39 us: paired(): call(prepare_weights_kernel, [SMEM] + [VMEM] * 2, [VMEM] * 3, [array(PAD...]
  transfers between devices with their start and end apart: 36 -> 36, of which waited for: 17 -> 18; matrix products, arithmetic and copies ran while one was open for 4% -> 4% of each run, Pallas kernels for 19% -> 19%
where the time goes in v2:
time: 181 us
  waiting for transfers between devices  69.5 us (38%)
  Pallas kernels  56.9 us (31%)
  starting transfers between devices  35.3 us (20%)
  local copies, waits for them, and re-layouts  9.19 us (5%)
  other arithmetic  8.58 us (5%)
    ppermute x3, waiting for transfers between devices, onward(): return lax.ppermute(value, 'expert', [(i, (i + 1) % 4) for i in range(4)])  37.4 us
    ppermute x27, waiting for transfers between devices, swap(): return lambda value: lax.ppermute(value, 'dp', pairs)  23.3 us
    ppermute x27, starting transfers between devices, swap(): return lambda value: lax.ppermute(value, 'dp', pairs)  20.6 us
    pallas_call x1, Pallas kernels, paired(): call(functools.partial(forward_kernel, scale), [SMEM] + [ANY] * 16, [ANY]...  18.3 us
    pallas_call x1, Pallas kernels, paired(): call(functools.partial(up_grad_kernel, scale), [SMEM] + [ANY] * 17, [ANY]...  12.9 us
    ppermute x6, starting transfers between devices, backward(): return lax.ppermute(value, 'expert', [(i, (i + 3) % 4) for i in range(4)])  11.6 us
    pallas_call x1, Pallas kernels, paired(): call(functools.partial(gate_grad_kernel, scale), [SMEM] + [ANY] * 19, [AN...  10.7 us
    unnamed x82, local copies, waits for them, and re-layouts  9.19 us
  transfers between devices with their start and end apart: 36, of which 18 were waited for; matrix products, arithmetic and copies ran while one was open for 4% of the time, Pallas kernels for 19%

profile of v2, /device:TPU:0, one launch (start us, length us, event | category | flops | bytes accessed | tf_op | source)
XLA Modules:
  0.0 180.6 jit_solution(14265872121293603859)
XLA Ops:
  0.6 2.4 %shard_map.95.refs_9_.refs_12_ = bf16[128,3072]{1,0:T(8,128)(2,1)} custom-call(bf16[1440,128]{1,0:T(8,128)(2,1)} %bitcast.42, bf16[1440,128]{1,0:T(8,128)(2,1)} %bitcast.43, s32[2,128]{1,0:T(2,128)} %bitcast.46, f32[2,128]{1,0:T(2,128)} %bitcast.47), custom_call_target="tpu_custom_call" | custom-call | flops 1000 | bytes 1000 | tf_op jit(solution)/shard_map/pallas_call | solution.py:434
  3.0 3.0 %collective-permute-start.8 = (bf16[128,3072]{1,0:T(8,128)(2,1)}, bf16[128,3072]{1,0:T(8,128)(2,1)S(1)}, u32[]{:S(2)}, u32[]{:S(2)}) collective-permute-start(bf16[128,3072]{1,0:T(8,128)(2,1)} %shard_map.95.refs_9_.refs_12_), channel_id=1, source_target_pairs={{0,1},{1,2},{2,3},{3,0},{4,5},{5,6},{6,7},{7,4},{8,9},{9,10},{10,1... | collective-permute-start | bytes 2359304 | tf_op jit(solution)/shard_map/ppermute | solution.py:420
  6.7 3.4 %shard_map.93 = (bf16[272,1536]{1,0:T(8,128)(2,1)}, bf16[192,1536]{1,0:T(8,128)(2,1)}, bf16[80,1536]{1,0:T(8,128)(2,1)}) custom-call(s32[3]{0:T(128)} %pad_add_fusion.spot.refs_0_, bf16[180,2880]{1,0:T(8,128)(2,1)} %bitcast.41, bf16[180,1440]{1,0:T(8,128)(2,1)} %bitcast.37), custom_call_target="tpu_custom_call" | custom-call | flops 1000 | bytes 1000 | tf_op jit(solution)/shard_map/pallas_call | solution.py:437
  10.1 1.5 collective-permute-start.1
  11.6 1.5 collective-permute-start
  13.1 12.8 %collective-permute-done.8.refs_10_.refs_13_ = bf16[128,3072]{1,0:T(8,128)(2,1)S(1)} collective-permute-done((bf16[128,3072]{1,0:T(8,128)(2,1)}, bf16[128,3072]{1,0:T(8,128)(2,1)S(1)}, u32[]{:S(2)}, u32[]{:S(2)}) %collective-permute-start.8) | collective-permute-done | bytes 786464 | tf_op jit(solution)/shard_map/ppermute | solution.py:420
  25.9 2.2 %collective-permute-done.2.other = bf16[192,1536]{1,0:T(8,128)(2,1)S(1)} collective-permute-done((bf16[192,1536]{1,0:T(8,128)(2,1)}, bf16[192,1536]{1,0:T(8,128)(2,1)S(1)}, u32[]{:S(2)}, u32[]{:S(2)}) %collective-permute-start.2) | collective-permute-done | bytes 589856 | tf_op jit(solution)/shard_map/ppermute | solution.py:415
  33.6 12.8 %collective-permute-done.9.refs_11_.refs_14_ = bf16[128,3072]{1,0:T(8,128)(2,1)S(1)} collective-permute-done((bf16[128,3072]{1,0:T(8,128)(2,1)S(1)}, bf16[128,3072]{1,0:T(8,128)(2,1)S(1)}, u32[]{:S(2)}, u32[]{:S(2)}) %collective-permute-start.9) | collective-permute-done | bytes 786464 | tf_op jit(solution)/shard_map/ppermute | solution.py:420
  46.4 4.0 %collective-permute-done.5.refs_7_ = bf16[272,1536]{1,0:T(8,128)(2,1)S(1)} collective-permute-done((bf16[272,1536]{1,0:T(8,128)(2,1)S(1)}, bf16[272,1536]{1,0:T(8,128)(2,1)S(1)}, u32[]{:S(2)}, u32[]{:S(2)}) %collective-permute-start.5) | collective-permute-done | bytes 835616 | tf_op jit(solution)/shard_map/ppermute | solution.py:415
  54.2 11.8 %collective-permute-done.10.refs_12_.refs_15_ = bf16[128,3072]{1,0:T(8,128)(2,1)S(1)} collective-permute-done((bf16[128,3072]{1,0:T(8,128)(2,1)S(1)}, bf16[128,3072]{1,0:T(8,128)(2,1)S(1)}, u32[]{:S(2)}, u32[]{:S(2)}) %collective-permute-start.10) | collective-permute-done | bytes 786464 | tf_op jit(solution)/shard_map/ppermute | solution.py:420
  66.0 3.2 %collective-permute-done.6.refs_4_ = bf16[272,1536]{1,0:T(8,128)(2,1)S(1)} collective-permute-done((bf16[272,1536]{1,0:T(8,128)(2,1)S(1)}, bf16[272,1536]{1,0:T(8,128)(2,1)S(1)}, u32[]{:S(2)}, u32[]{:S(2)}) %collective-permute-start.6) | collective-permute-done | bytes 835616 | tf_op jit(solution)/shard_map/ppermute | solution.py:415
  70.5 18.3 %shard_map.96 = (bf16[1024,768]{1,0:T(8,128)(2,1)}, bf16[1024,768]{1,0:T(8,128)(2,1)}, bf16[1024,1536]{1,0:T(8,128)(2,1)}, bf16[512,1536]{1,0:T(8,128)(2,1)}, bf...) custom-call(s32[3]{0:T(128)S(1)} %copy-done.22, ...), custom_call_target="tpu_custom_call" | custom-call | flops 30000001024 | bytes 1000 | tf_op jit(solution)/shard_map/pallas_call | solution.py:457
  88.9 1.6 collective-permute-start.14
  93.0 5.4 %collective-permute-start.17 = (bf16[128,1536]{1,0:T(8,128)(2,1)S(1)}, bf16[128,1536]{1,0:T(8,128)(2,1)S(1)}, u32[]{:S(2)}, u32[]{:S(2)}) collective-permute-start(bf16[128,1536]{1,0:T(8,128)(2,1)S(1)} %add_convert_fusion.5), channel_id=1, source_target_pairs={{0,3},{1,0},{2,1},{3,2},{4,7},{5,4},{6,5},{7,6},{8,11},{9,8},{10,9... | collective-permute-start | bytes 1179656 | tf_op jit(solution)/shard_map/ppermute | solution.py:423
  99.5 10.7 %shard_map.97 = (bf16[1024,1536]{1,0:T(8,128)(2,1)}, bf16[2,192,768]{2,1,0:T(8,128)(2,1)S(1)}, bf16[2,192,768]{2,1,0:T(8,128)(2,1)S(1)}, bf16[2,192,768]{2,1,0:T(8,128)(2,1)S(1)}, bf16[2,192,768]{2,1,0:T(8,128)(2,1)S(1)}) custom-call(s32[3]{0:T(128)S(1)} %copy-done.22, bf16[272,1536]{1,0:T(8,128)(2,1)} %get-tuple-element.70.refs_1_, ...), custom_call_target="tpu_custom_call" | custom-call | flops 30000001024 | bytes 1000 | tf_op jit(solution)/shard_map/pallas_call | solution.py:498
  116.3 12.9 %shard_map.98 = (bf16[512,1536]{1,0:T(8,128)(2,1)}, bf16[128,1536]{1,0:T(8,128)(2,1)S(1)}, bf16[384,1536]{1,0:T(8,128)(2,1)}, bf16[3,192,768]{2,1,0:T(8,128)(2,1...) custom-call(s32[3]{0:T(128)S(1)} %copy-done.22, ...), custom_call_target="tpu_custom_call" | custom-call | flops 30000001024 | bytes 1000 | tf_op jit(solution)/shard_map/pallas_call | solution.py:513
  129.3 2.9 %collective-permute-done.22.got_a = bf16[2,192,768]{2,1,0:T(8,128)(2,1)S(1)} collective-permute-done((bf16[2,192,768]{2,1,0:T(8,128)(2,1)S(1)}, bf16[2,192,768]{2,1,0:T(8,128)(2,1)S(1)}, u32[]{:S(2)}, u32[]{:S(2)}) %collective-permute-start.22) | collective-permute-done | bytes 589856 | tf_op jit(solution)/shard_map/ppermute | solution.py:415
  140.1 8.8 %collective-permute-done.32 = bf16[128,1536]{1,0:T(8,128)(2,1)S(1)} collective-permute-done((bf16[128,1536]{1,0:T(8,128)(2,1)S(1)}, bf16[128,1536]{1,0:T(8,128)(2,1)S(1)}, u32[]{:S(2)}, u32[]{:S(2)}) %collective-permute-start.32) | collective-permute-done | bytes 393248 | tf_op jit(solution)/shard_map/ppermute | solution.py:423
  150.0 2.7 %collective-permute-start.33 = (bf16[128,1536]{1,0:T(8,128)(2,1)}, bf16[128,1536]{1,0:T(8,128)(2,1)}, u32[]{:S(2)}, u32[]{:S(2)}) collective-permute-start(bf16[128,1536]{1,0:T(8,128)(2,1)} %get-tuple-element.141), channel_id=1, source_target_pairs={{0,3},{1,0},{2,1},{3,2},{4,7},{5,4},{6,5},{7,6},{8,11},{9,8},{10,9... | collective-permute-start | bytes 1179656 | tf_op jit(solution)/shard_map/ppermute | solution.py:423
  160.8 1.6 fusion.5
  164.6 1.9 %shard_map.101 = bf16[1440,128]{1,0:T(8,128)(2,1)} custom-call(f32[128,1536]{1,0:T(8,128)S(1)} %get-tuple-element.142.keep, bf16[128,1536]{1,0:T(8,128)(2,1)} %collective-permute-done.26.got), custom_call_target="tpu_custom_call" | custom-call | flops 1000 | bytes 1000 | tf_op jit(solution)/shard_map/pallas_call | solution.py:541
  169.2 2.7 %collective-permute-done.28 = bf16[192,768]{1,0:T(8,128)(2,1)S(1)} collective-permute-done((bf16[192,768]{1,0:T(8,128)(2,1)S(1)}, bf16[192,768]{1,0:T(8,128)(2,1)S(1)}, u32[]{:S(2)}, u32[]{:S(2)}) %collective-permute-start.28) | collective-permute-done | bytes 294944 | tf_op jit(solution)/shard_map/ppermute | solution.py:415
  174.4 1.6 collective-permute-done.35.up_far
  176.0 3.7 %shard_map.103 = f32[180,1,2880]{2,1,0:T(1,128)} custom-call(s32[3]{0:T(128)S(1)} %copy-done.22, f32[192,768]{1,0:T(8,128)S(1)} %get-tuple-element.131.gate_keep, bf16[192,768]{1,0:T(8,128)(2,1)S(1)} %collective-permute-done.29.gate_far, f32[192,768]{1,0:T(8,128)S(1)} %get-tuple-element.139.up_keep, bf16[192,768]{1,0:T(8,128)(2,1)S(1)} %collective-permute-done.35.up_far), custom_call_target="tpu_custom_call" | custom-call | flops 1000 | bytes 1000 | tf_op jit(solution)/shard_map/pallas_call | solution.py:561
  (152 shorter events, 46.0 us)
Async XLA Ops:
  3.0 22.9 %collective-permute-start.8 = (bf16[128,3072]{1,0:T(8,128)(2,1)}, bf16[128,3072]{1,0:T(8,128)(2,1)S(1)}, u32[]{:S(2)}, u32[]{:S(2)}) collective-permute-start(bf16[128,3072]{1,0:T(8,128)(2,1)} %shard_map.95.refs_9_.refs_12_), channel_id=1, source_target_pairs={{0,1},{1,2},{2,3},{3,0},{4,5},{5,6},{6,7},{7,4},{8,9},{9,10},{10,1... | collective-permute-start | bytes 2359304 | tf_op jit(solution)/shard_map/ppermute | solution.py:420
  10.1 20.3 %collective-permute-start.1 = (bf16[272,1536]{1,0:T(8,128)(2,1)}, bf16[272,1536]{1,0:T(8,128)(2,1)S(1)}, u32[]{:S(2)}, u32[]{:S(2)}) collective-permute-start(bf16[272,1536]{1,0:T(8,128)(2,1)} %get-tuple-element.70.refs_1_), channel_id=1, source_target_pairs={{0,16},{4,20},{8,24},{12,28},{16,0},{20,4},{24,8},{28,12},{1,17},{... | collective-permute-start | bytes 2506760 | tf_op jit(solution)/shard_map/ppermute | solution.py:415
  11.6 20.0 %collective-permute-start = (bf16[272,1536]{1,0:T(8,128)(2,1)}, bf16[272,1536]{1,0:T(8,128)(2,1)S(1)}, u32[]{:S(2)}, u32[]{:S(2)}) collective-permute-start(bf16[272,1536]{1,0:T(8,128)(2,1)} %get-tuple-element.70.refs_1_), channel_id=1, source_target_pairs={{0,8},{4,12},{8,0},{12,4},{16,24},{20,28},{24,16},{28,20},{1,9},{5... | collective-permute-start | bytes 2506760 | tf_op jit(solution)/shard_map/ppermute | solution.py:415
  13.1 16.0 %collective-permute-start.3 = (bf16[128,3072]{1,0:T(8,128)(2,1)S(1)}, bf16[128,3072]{1,0:T(8,128)(2,1)S(1)}, u32[]{:S(2)}, u32[]{:S(2)}) collective-permute-start(bf16[128,3072]{1,0:T(8,128)(2,1)S(1)} %copy-done.12), channel_id=1, source_target_pairs={{0,4},{4,0},{8,12},{12,8},{16,20},{20,16},{24,28},{28,24},{1,5},{5... | collective-permute-start | bytes 2359304 | tf_op jit(solution)/shard_map/ppermute | solution.py:415
  25.9 20.5 %collective-permute-start.9 = (bf16[128,3072]{1,0:T(8,128)(2,1)S(1)}, bf16[128,3072]{1,0:T(8,128)(2,1)S(1)}, u32[]{:S(2)}, u32[]{:S(2)}) collective-permute-start(bf16[128,3072]{1,0:T(8,128)(2,1)S(1)} %collective-permute-done.8.refs_10_.refs_13_), channel_id=1, source_target_pairs={{0,1},{1,2},{2,3},{3,0},{4,5},{5,6},{6,7},{7,4},{8,9},{9,10},{10,1... | collective-permute-start | bytes 2359304 | tf_op jit(solution)/shard_map/ppermute | solution.py:420
  31.6 18.8 %collective-permute-start.5 = (bf16[272,1536]{1,0:T(8,128)(2,1)S(1)}, bf16[272,1536]{1,0:T(8,128)(2,1)S(1)}, u32[]{:S(2)}, u32[]{:S(2)}) collective-permute-start(bf16[272,1536]{1,0:T(8,128)(2,1)S(1)} %shard_map.94.refs_5_), channel_id=1, source_target_pairs={{0,16},{4,20},{8,24},{12,28},{16,0},{20,4},{24,8},{28,12},{1,17},{... | collective-permute-start | bytes 2506760 | tf_op jit(solution)/shard_map/ppermute | solution.py:415
  32.1 19.0 %collective-permute-start.4 = (bf16[272,1536]{1,0:T(8,128)(2,1)S(1)}, bf16[272,1536]{1,0:T(8,128)(2,1)S(1)}, u32[]{:S(2)}, u32[]{:S(2)}) collective-permute-start(bf16[272,1536]{1,0:T(8,128)(2,1)S(1)} %shard_map.94.refs_5_), channel_id=1, source_target_pairs={{0,8},{4,12},{8,0},{12,4},{16,24},{20,28},{24,16},{28,20},{1,9},{5... | collective-permute-start | bytes 2506760 | tf_op jit(solution)/shard_map/ppermute | solution.py:415
  46.4 19.6 %collective-permute-start.10 = (bf16[128,3072]{1,0:T(8,128)(2,1)S(1)}, bf16[128,3072]{1,0:T(8,128)(2,1)S(1)}, u32[]{:S(2)}, u32[]{:S(2)}) collective-permute-start(bf16[128,3072]{1,0:T(8,128)(2,1)S(1)} %collective-permute-done.9.refs_11_.refs_14_), channel_id=1, source_target_pairs={{0,1},{1,2},{2,3},{3,0},{4,5},{5,6},{6,7},{7,4},{8,9},{9,10},{10,1... | collective-permute-start | bytes 2359304 | tf_op jit(solution)/shard_map/ppermute | solution.py:420
  51.1 18.1 %collective-permute-start.6 = (bf16[272,1536]{1,0:T(8,128)(2,1)S(1)}, bf16[272,1536]{1,0:T(8,128)(2,1)S(1)}, u32[]{:S(2)}, u32[]{:S(2)}) collective-permute-start(bf16[272,1536]{1,0:T(8,128)(2,1)S(1)} %collective-permute-done.refs_2_), channel_id=1, source_target_pairs={{0,16},{4,20},{8,24},{12,28},{16,0},{20,4},{24,8},{28,12},{1,17},{... | collective-permute-start | bytes 2506760 | tf_op jit(solution)/shard_map/ppermute | solution.py:415
  52.2 17.4 %collective-permute-start.7 = (bf16[272,1536]{1,0:T(8,128)(2,1)S(1)}, bf16[272,1536]{1,0:T(8,128)(2,1)S(1)}, u32[]{:S(2)}, u32[]{:S(2)}) collective-permute-start(bf16[272,1536]{1,0:T(8,128)(2,1)S(1)} %collective-permute-done.5.refs_7_), channel_id=1, source_target_pairs={{0,8},{4,12},{8,0},{12,4},{16,24},{20,28},{24,16},{28,20},{1,9},{5... | collective-permute-start | bytes 2506760 | tf_op jit(solution)/shard_map/ppermute | solution.py:415
  88.9 21.3 %collective-permute-start.14 = (bf16[2,96,1536]{2,1,0:T(8,128)(2,1)S(1)}, bf16[2,96,1536]{2,1,0:T(8,128)(2,1)S(1)}, u32[]{:S(2)}, u32[]{:S(2)}) collective-permute-start(bf16[2,96,1536]{2,1,0:T(8,128)(2,1)S(1)} %get-tuple-element.80), channel_id=1, source_target_pairs={{0,8},{4,12},{8,0},{12,4},{16,24},{20,28},{24,16},{28,20},{1,9},{5... | collective-permute-start | bytes 1769480 | tf_op jit(solution)/shard_map/ppermute | solution.py:415
  90.5 19.8 %collective-permute-start.15 = (bf16[2,96,1536]{2,1,0:T(8,128)(2,1)S(1)}, bf16[2,96,1536]{2,1,0:T(8,128)(2,1)S(1)}, u32[]{:S(2)}, u32[]{:S(2)}) collective-permute-start(bf16[2,96,1536]{2,1,0:T(8,128)(2,1)S(1)} %get-tuple-element.81), channel_id=1, source_target_pairs={{0,16},{4,20},{8,24},{12,28},{16,0},{20,4},{24,8},{28,12},{1,17},{... | collective-permute-start | bytes 1769480 | tf_op jit(solution)/shard_map/ppermute | solution.py:415
  91.9 18.4 %collective-permute-start.18 = (bf16[384,1536]{1,0:T(8,128)(2,1)}, bf16[384,1536]{1,0:T(8,128)(2,1)S(1)}, u32[]{:S(2)}, u32[]{:S(2)}) collective-permute-start(bf16[384,1536]{1,0:T(8,128)(2,1)} %get-tuple-element.92), channel_id=1, source_target_pairs={{0,4},{4,0},{8,12},{12,8},{16,20},{20,16},{24,28},{28,24},{1,5},{5... | collective-permute-start | bytes 3538952 | tf_op jit(solution)/shard_map/ppermute | solution.py:415
  93.0 17.3 %collective-permute-start.17 = (bf16[128,1536]{1,0:T(8,128)(2,1)S(1)}, bf16[128,1536]{1,0:T(8,128)(2,1)S(1)}, u32[]{:S(2)}, u32[]{:S(2)}) collective-permute-start(bf16[128,1536]{1,0:T(8,128)(2,1)S(1)} %add_convert_fusion.5), channel_id=1, source_target_pairs={{0,3},{1,0},{2,1},{3,2},{4,7},{5,4},{6,5},{7,6},{8,11},{9,8},{10,9... | collective-permute-start | bytes 1179656 | tf_op jit(solution)/shard_map/ppermute | solution.py:423
  110.4 18.9 %collective-permute-start.21 = (bf16[96,1536]{1,0:T(8,128)(2,1)S(1)}, bf16[96,1536]{1,0:T(8,128)(2,1)S(1)}, u32[]{:S(2)}, u32[]{:S(2)}) collective-permute-start(bf16[96,1536]{1,0:T(8,128)(2,1)S(1)} %fusion.2), channel_id=1, source_target_pairs={{0,8},{4,12},{8,0},{12,4},{16,24},{20,28},{24,16},{28,20},{1,9},{5... | collective-permute-start | bytes 884744 | tf_op jit(solution)/shard_map/ppermute | solution.py:415
  111.0 18.2 %collective-permute-start.20 = (bf16[96,1536]{1,0:T(8,128)(2,1)S(1)}, bf16[96,1536]{1,0:T(8,128)(2,1)S(1)}, u32[]{:S(2)}, u32[]{:S(2)}) collective-permute-start(bf16[96,1536]{1,0:T(8,128)(2,1)S(1)} %fusion.1), channel_id=1, source_target_pairs={{0,16},{4,20},{8,24},{12,28},{16,0},{20,4},{24,8},{28,12},{1,17},{... | collective-permute-start | bytes 884744 | tf_op jit(solution)/shard_map/ppermute | solution.py:415
  112.4 16.9 %collective-permute-start.19 = (bf16[128,1536]{1,0:T(8,128)(2,1)S(1)}, bf16[128,1536]{1,0:T(8,128)(2,1)S(1)}, u32[]{:S(2)}, u32[]{:S(2)}) collective-permute-start(bf16[128,1536]{1,0:T(8,128)(2,1)S(1)} %add_convert_fusion.4), channel_id=1, source_target_pairs={{0,3},{1,0},{2,1},{3,2},{4,7},{5,4},{6,5},{7,6},{8,11},{9,8},{10,9... | collective-permute-start | bytes 1179656 | tf_op jit(solution)/shard_map/ppermute | solution.py:423
  113.5 18.7 %collective-permute-start.22 = (bf16[2,192,768]{2,1,0:T(8,128)(2,1)S(1)}, bf16[2,192,768]{2,1,0:T(8,128)(2,1)S(1)}, u32[]{:S(2)}, u32[]{:S(2)}) collective-permute-start(bf16[2,192,768]{2,1,0:T(8,128)(2,1)S(1)} %get-tuple-element.104), channel_id=1, source_target_pairs={{0,8},{4,12},{8,0},{12,4},{16,24},{20,28},{24,16},{28,20},{1,9},{5... | collective-permute-start | bytes 1769480 | tf_op jit(solution)/shard_map/ppermute | solution.py:415
  115.0 17.6 %collective-permute-start.23 = (bf16[2,192,768]{2,1,0:T(8,128)(2,1)S(1)}, bf16[2,192,768]{2,1,0:T(8,128)(2,1)S(1)}, u32[]{:S(2)}, u32[]{:S(2)}) collective-permute-start(bf16[2,192,768]{2,1,0:T(8,128)(2,1)S(1)} %get-tuple-element.105), channel_id=1, source_target_pairs={{0,16},{4,20},{8,24},{12,28},{16,0},{20,4},{24,8},{28,12},{1,17},{... | collective-permute-start | bytes 1769480 | tf_op jit(solution)/shard_map/ppermute | solution.py:415
  135.0 13.8 %collective-permute-start.30 = (bf16[384,1536]{1,0:T(8,128)(2,1)S(1)}, bf16[384,1536]{1,0:T(8,128)(2,1)S(1)}, u32[]{:S(2)}, u32[]{:S(2)}) collective-permute-start(bf16[384,1536]{1,0:T(8,128)(2,1)S(1)} %copy-done.30), channel_id=1, source_target_pairs={{0,4},{4,0},{8,12},{12,8},{16,20},{20,16},{24,28},{28,24},{1,5},{5... | collective-permute-start | bytes 3538952 | tf_op jit(solution)/shard_map/ppermute | solution.py:415
  137.8 22.5 %collective-permute-start.24 = (bf16[3,192,768]{2,1,0:T(8,128)(2,1)}, bf16[3,192,768]{2,1,0:T(8,128)(2,1)}, u32[]{:S(2)}, u32[]{:S(2)}) collective-permute-start(bf16[3,192,768]{2,1,0:T(8,128)(2,1)} %get-tuple-element.118), channel_id=1, source_target_pairs={{0,8},{4,12},{8,0},{12,4},{16,24},{20,28},{24,16},{28,20},{1,9},{5... | collective-permute-start | bytes 2654216 | tf_op jit(solution)/shard_map/ppermute | solution.py:415
  139.3 21.4 %collective-permute-start.25 = (bf16[3,192,768]{2,1,0:T(8,128)(2,1)}, bf16[3,192,768]{2,1,0:T(8,128)(2,1)}, u32[]{:S(2)}, u32[]{:S(2)}) collective-permute-start(bf16[3,192,768]{2,1,0:T(8,128)(2,1)} %get-tuple-element.119), channel_id=1, source_target_pairs={{0,16},{4,20},{8,24},{12,28},{16,0},{20,4},{24,8},{28,12},{1,17},{... | collective-permute-start | bytes 2654216 | tf_op jit(solution)/shard_map/ppermute | solution.py:415
  140.0 20.3 %collective-permute-start.26 = (bf16[128,1536]{1,0:T(8,128)(2,1)}, bf16[128,1536]{1,0:T(8,128)(2,1)}, u32[]{:S(2)}, u32[]{:S(2)}) collective-permute-start(bf16[128,1536]{1,0:T(8,128)(2,1)} %get-tuple-element.120), channel_id=1, source_target_pairs={{0,3},{1,0},{2,1},{3,2},{4,7},{5,4},{6,5},{7,6},{8,11},{9,8},{10,9... | collective-permute-start | bytes 1179656 | tf_op jit(solution)/shard_map/ppermute | solution.py:423
  150.0 16.5 %collective-permute-start.33 = (bf16[128,1536]{1,0:T(8,128)(2,1)}, bf16[128,1536]{1,0:T(8,128)(2,1)}, u32[]{:S(2)}, u32[]{:S(2)}) collective-permute-start(bf16[128,1536]{1,0:T(8,128)(2,1)} %get-tuple-element.141), channel_id=1, source_target_pairs={{0,3},{1,0},{2,1},{3,2},{4,7},{5,4},{6,5},{7,6},{8,11},{9,8},{10,9... | collective-permute-start | bytes 1179656 | tf_op jit(solution)/shard_map/ppermute | solution.py:423
  (53 other events, 557.0 us)
